TPU v7x, 32 devices: a whole 2x2x4 slice. The times are simulated.
32 devices in a mesh: dp: 8 (over z, y), mp: 4 (over x, core).
Axes of the slice: x: 2, y: 2, z: 4, core: 2. Of those that a mesh axis runs over, the one named last changes fastest.
Arguments:
- tokens: bfloat16 [32768, 1152], P(('dp', 'mp')), may hold values from -6 to 6
- condition: bfloat16 [16, 1152], P('dp'), may hold values from -6 to 6
- grid_rows: int32 [128], P('dp'), may hold values from 12 to 20, as said below
- grid_cols: int32 [128], P('dp'), may hold values from 12 to 20, as said below
- frame_start: int32 [128], P('dp'), may hold values from 0 to 3856, as said below
- frame_item: int32 [128], P('dp'), may hold values from 0 to 1, as said below
- group_frames: int32 [8], P('dp'), may hold values from 8 to 16, as said below
- w_qkv: bfloat16 [1152, 3, 1152], P(None, None, 'mp'), may hold values from -0.1875 to 0.1875
- qv_bias: bfloat16 [2, 1152], P(None, 'mp'), may hold values from -3 to 3
- w_out: bfloat16 [1152, 1152], P('mp'), may hold values from -1.5 to 1.5
- b_out: bfloat16 [1152], replicated, may hold values from -2 to 2
- w_up: bfloat16 [1152, 4608], P(None, 'mp'), may hold values from -0.1875 to 0.1875
- b_up: bfloat16 [4608], P('mp'), may hold values from -3 to 3
- w_down: bfloat16 [4608, 1152], P('mp'), may hold values from -0.09375 to 0.09375
- b_down: bfloat16 [1152], replicated, may hold values from -2 to 2
- w_ada: bfloat16 [1152, 6, 1152], P(None, None, 'mp'), may hold values from -0.1875 to 0.1875
- b_ada: bfloat16 [6, 1152], P(None, 'mp'), may hold values from -2 to 2
- cotangent: bfloat16 [32768, 1152], P(('dp', 'mp')), may hold values from -6 to 6
Outputs:
- output: bfloat16 [32768, 1152], P(('dp', 'mp'))
- grad_tokens: bfloat16 [32768, 1152], P(('dp', 'mp'))
- grad_condition: float32 [16, 1152], P('dp')
- grad_w_qkv: float32 [1152, 3, 1152], P(None, None, 'mp')
- grad_qv_bias: float32 [2, 1152], P(None, 'mp')
- grad_w_out: float32 [1152, 1152], P('mp')
- grad_b_out: float32 [1152], replicated
- grad_w_up: float32 [1152, 4608], P(None, 'mp')
- grad_b_up: float32 [4608], P('mp')
- grad_w_down: float32 [4608, 1152], P('mp')
- grad_b_down: float32 [1152], replicated
- grad_w_ada: float32 [1152, 6, 1152], P(None, None, 'mp')
- grad_b_ada: float32 [6, 1152], P(None, 'mp')
Inputs may be any that keep to these rules, and one draw needn't show every extreme that they name: `grid_rows`: each frame slot's grid is one of 16 x 16, 12 x 20, 20 x 12, 14 x 18 (rows x columns). `grid_cols`: paired with grid_rows as stated there. `frame_start`: slot k of a group starts at a row from k * 256 to (k + 1) * 256 - grid_rows[k] * grid_cols[k], so that it ends within its own 256 rows. `frame_item`: slots 0 and 1 of a group name different videos. `group_frames`: some group uses all of the slots and some group exactly half of them, rounded down; used slots come first.
All inputs are finite; a program needn't handle non-finite values.
Results may differ from a plain program's by a relative error of at most 0.02.
Values may be sent and summed in bfloat16 or wider, within the bound.
A program may use at most 448 MiB of HBM per device.

v0:
```python
import jax
import jax.numpy as jnp
from jax import lax
from jax.sharding import PartitionSpec as P

HEAD = 72
SLOT = 256


precise = lax.Precision.HIGHEST
epsilon = 1e-06


def frame_tables(grid_rows, grid_cols, frame_start, frame_item, used, length):
    rows = jnp.arange(length, dtype=jnp.int32)[:, None]
    slots = jnp.arange(grid_rows.shape[0], dtype=jnp.int32)[None, :]
    ends = (frame_start + grid_rows * grid_cols)[None, :]
    inside = (rows >= frame_start[None, :]) & (rows < ends) & (slots < used)
    frame_id = jnp.sum(jnp.where(inside, slots + 1, 0), axis=1) - 1
    item_id = jnp.sum(jnp.where(inside, frame_item[None, :], 0), axis=1)
    return (frame_id, item_id)


def allowed_pairs(frames):
    span = frames.shape[-1]
    place = jnp.arange(span, dtype=jnp.int32)
    same = (frames[..., :, None] == frames[..., None, :]) & (frames[..., :, None] >= 0)
    return same | (place[:, None] == place[None, :])


def layer_norm(values):
    centred = values - jnp.mean(values, axis=-1, keepdims=True)
    variance = jnp.mean(centred * centred, axis=-1, keepdims=True)
    return centred * lax.rsqrt(variance + epsilon)


def modulate(values, shift, scale):
    return layer_norm(values) * (1.0 + scale) + shift


def row_inner(left, right):
    return lax.dot_general(
        left, right, (((0,), (0,)), ((), ())), preferred_element_type=jnp.float32
    )


def col_inner(left, right):
    return lax.dot_general(
        left, right, (((1,), (1,)), ((), ())), preferred_element_type=jnp.float32
    )


def gelu_tanh(values):
    return jax.nn.gelu(values, approximate=True)


def shards(
    tokens,
    condition,
    grid_rows,
    grid_cols,
    frame_start,
    frame_item,
    group_frames,
    w_qkv,
    qv_bias,
    w_out,
    b_out,
    w_up,
    b_up,
    w_down,
    b_down,
    w_ada,
    b_ada,
    cotangent,
):
    own_rows, width = tokens.shape
    group_rows = own_rows * lax.axis_size("mp")
    local_width = w_qkv.shape[2]
    local_heads = local_width // HEAD
    items = condition.shape[0]
    span = 2 * SLOT
    blocks = group_rows // span
    scale = HEAD ** (-0.5)
    frame_id, item_id = frame_tables(
        grid_rows, grid_cols, frame_start, frame_item, group_frames[0], group_rows
    )
    first = lax.axis_index("mp") * own_rows
    own_items = lax.dynamic_slice_in_dim(item_id, first, own_rows)
    chooser = (own_items[:, None] == jnp.arange(items, dtype=jnp.int32)[None, :]).astype(
        jnp.float32
    )
    cond_value = condition.astype(jnp.float32)
    act_low = jax.nn.silu(cond_value).astype(jnp.bfloat16)
    ada_flat = w_ada.reshape(width, -1)
    ada_local = jnp.dot(act_low, ada_flat, preferred_element_type=jnp.float32) + b_ada.reshape(
        -1
    ).astype(jnp.float32)
    ada_local = ada_local.reshape(items, 6, -1)
    modulation = lax.all_gather(ada_local, "mp", axis=2, tiled=True)
    per_token = jnp.dot(chooser, modulation.reshape(items, -1), precision=precise).reshape(
        own_rows, 6, width
    )
    shift_one, scale_one, gate_one = (per_token[:, 0], per_token[:, 1], per_token[:, 2])
    shift_two, scale_two, gate_two = (per_token[:, 3], per_token[:, 4], per_token[:, 5])
    inputs = tokens.astype(jnp.float32)
    normed_one = modulate(inputs, shift_one, scale_one).astype(jnp.bfloat16)
    gathered_one = lax.all_gather(normed_one, "mp", axis=0, tiled=True)
    qkv_flat = w_qkv.reshape(width, -1)
    bias = jnp.stack([qv_bias[0], jnp.zeros_like(qv_bias[0]), qv_bias[1]]).astype(jnp.float32)
    projected = (
        jnp.dot(gathered_one, qkv_flat, preferred_element_type=jnp.float32).reshape(
            group_rows, 3, local_width
        )
        + bias[None]
    )
    projected = projected.astype(jnp.bfloat16)

    def to_blocks(values):
        return values.reshape(blocks, span, local_heads, HEAD)

    queries = to_blocks(projected[:, 0])
    keys = to_blocks(projected[:, 1])
    values = to_blocks(projected[:, 2])
    allowed = allowed_pairs(frame_id.reshape(blocks, span))[:, None]

    def raw_scores():
        scores = (
            jnp.einsum("bqhe,bkhe->bhqk", queries, keys, preferred_element_type=jnp.float32) * scale
        )
        return jnp.where(allowed, scores, -1e30)

    scores = raw_scores()
    peak = jnp.max(scores, axis=-1, keepdims=True)
    weights = jnp.exp(scores - peak)
    totals = jnp.sum(weights, axis=-1, keepdims=True)
    log_total = peak + jnp.log(totals)
    probs = (weights / totals).astype(jnp.bfloat16)
    attended = jnp.einsum("bhqk,bkhe->bqhe", probs, values, preferred_element_type=jnp.float32)
    attended = attended.reshape(group_rows, local_width).astype(jnp.bfloat16)
    branch_one = lax.psum_scatter(
        jnp.dot(attended, w_out, preferred_element_type=jnp.float32).astype(jnp.bfloat16),
        "mp",
        scatter_dimension=0,
        tiled=True,
    ).astype(jnp.float32) + b_out.astype(jnp.float32)
    middle = inputs + gate_one * branch_one
    normed_two = modulate(middle, shift_two, scale_two).astype(jnp.bfloat16)
    gathered_two = lax.all_gather(normed_two, "mp", axis=0, tiled=True)
    pre_act = jnp.dot(gathered_two, w_up, preferred_element_type=jnp.float32) + b_up.astype(
        jnp.float32
    )
    hidden = gelu_tanh(pre_act).astype(jnp.bfloat16)
    branch_two = lax.psum_scatter(
        jnp.dot(hidden, w_down, preferred_element_type=jnp.float32).astype(jnp.bfloat16),
        "mp",
        scatter_dimension=0,
        tiled=True,
    ).astype(jnp.float32) + b_down.astype(jnp.float32)
    output = (middle + gate_two * branch_two).astype(jnp.bfloat16)
    upstream = cotangent.astype(jnp.float32)
    grad_gate_two = upstream * branch_two
    grad_branch_two = (gate_two * upstream).astype(jnp.bfloat16)
    full_two = lax.all_gather(grad_branch_two, "mp", axis=0, tiled=True)
    grad_b_down = jnp.sum(full_two.astype(jnp.float32), axis=0)
    grad_w_down = row_inner(hidden, full_two)
    grad_hidden = col_inner(full_two, w_down)
    unused, pull_gelu = jax.vjp(gelu_tanh, pre_act)
    grad_pre = pull_gelu(grad_hidden)[0].astype(jnp.bfloat16)
    grad_b_up = jnp.sum(grad_pre.astype(jnp.float32), axis=0)
    grad_w_up = row_inner(gathered_two, grad_pre)
    grad_normed_two = lax.psum_scatter(
        col_inner(grad_pre, w_up).astype(jnp.bfloat16), "mp", scatter_dimension=0, tiled=True
    ).astype(jnp.float32)
    unused, pull_two = jax.vjp(modulate, middle, shift_two, scale_two)
    grad_mid_norm, grad_shift_two, grad_scale_two = pull_two(grad_normed_two)
    grad_middle = upstream + grad_mid_norm
    grad_gate_one = grad_middle * branch_one
    grad_branch_one = (gate_one * grad_middle).astype(jnp.bfloat16)
    full_one = lax.all_gather(grad_branch_one, "mp", axis=0, tiled=True)
    grad_b_out = jnp.sum(full_one.astype(jnp.float32), axis=0)
    grad_w_out = row_inner(attended, full_one)
    grad_attended = to_blocks(col_inner(full_one, w_out).astype(jnp.bfloat16))
    recomputed = jnp.exp(raw_scores() - log_total)
    grad_probs = jnp.einsum(
        "bqhe,bkhe->bhqk", grad_attended, values, preferred_element_type=jnp.float32
    )
    grad_values = jnp.einsum(
        "bhqk,bqhe->bkhe",
        recomputed.astype(jnp.bfloat16),
        grad_attended,
        preferred_element_type=jnp.float32,
    )
    rowdot = jnp.sum(grad_probs * recomputed, axis=-1, keepdims=True)
    grad_scores = (recomputed * (grad_probs - rowdot)).astype(jnp.bfloat16)
    grad_queries = (
        jnp.einsum("bhqk,bkhe->bqhe", grad_scores, keys, preferred_element_type=jnp.float32) * scale
    )
    grad_keys = (
        jnp.einsum("bhqk,bqhe->bkhe", grad_scores, queries, preferred_element_type=jnp.float32)
        * scale
    )
    grad_projected = jnp.stack(
        [
            grad_queries.reshape(group_rows, local_width),
            grad_keys.reshape(group_rows, local_width),
            grad_values.reshape(group_rows, local_width),
        ],
        axis=1,
    )
    grad_projected = grad_projected.astype(jnp.bfloat16)
    bias_sums = jnp.sum(grad_projected.astype(jnp.float32), axis=0)
    grad_qv_bias = jnp.stack([bias_sums[0], bias_sums[2]])
    grad_flat = grad_projected.reshape(group_rows, 3 * local_width)
    grad_w_qkv = row_inner(gathered_one, grad_flat).reshape(width, 3, local_width)
    grad_normed_one = lax.psum_scatter(
        col_inner(grad_flat, qkv_flat).astype(jnp.bfloat16), "mp", scatter_dimension=0, tiled=True
    ).astype(jnp.float32)
    unused, pull_one = jax.vjp(modulate, inputs, shift_one, scale_one)
    grad_in_norm, grad_shift_one, grad_scale_one = pull_one(grad_normed_one)
    grad_tokens = (grad_middle + grad_in_norm).astype(jnp.bfloat16)
    per_token_grad = jnp.stack(
        [
            grad_shift_one,
            grad_scale_one,
            grad_gate_one,
            grad_shift_two,
            grad_scale_two,
            grad_gate_two,
        ],
        axis=1,
    )
    item_grad = lax.dot_general(
        chooser, per_token_grad.reshape(own_rows, -1), (((0,), (0,)), ((), ())), precision=precise
    ).reshape(items, 6, width)
    grad_ada = lax.psum_scatter(
        item_grad.astype(jnp.bfloat16), "mp", scatter_dimension=2, tiled=True
    ).astype(jnp.float32)
    grad_ada_flat = grad_ada.reshape(items, -1)
    grad_w_ada = lax.dot_general(
        act_low.astype(jnp.float32), grad_ada_flat, (((0,), (0,)), ((), ())), precision=precise
    ).reshape(width, 6, -1)
    grad_b_ada = jnp.sum(grad_ada, axis=0)
    cond_term = lax.dot_general(
        grad_ada_flat, ada_flat.astype(jnp.float32), (((1,), (1,)), ((), ())), precision=precise
    )
    grad_act = lax.psum(cond_term, "mp")
    unused, pull_silu = jax.vjp(jax.nn.silu, cond_value)
    grad_condition = pull_silu(grad_act)[0]
    (
        grad_w_qkv,
        grad_qv_bias,
        grad_w_out,
        grad_b_out,
        grad_w_up,
        grad_b_up,
        grad_w_down,
        grad_b_down,
        grad_w_ada,
        grad_b_ada,
    ) = (
        lax.psum(grad_w_qkv.astype(jnp.bfloat16), "dp").astype(jnp.float32),
        lax.psum(grad_qv_bias.astype(jnp.bfloat16), "dp").astype(jnp.float32),
        lax.psum(grad_w_out.astype(jnp.bfloat16), "dp").astype(jnp.float32),
        lax.psum(grad_b_out.astype(jnp.bfloat16), "dp").astype(jnp.float32),
        lax.psum(grad_w_up.astype(jnp.bfloat16), "dp").astype(jnp.float32),
        lax.psum(grad_b_up.astype(jnp.bfloat16), "dp").astype(jnp.float32),
        lax.psum(grad_w_down.astype(jnp.bfloat16), "dp").astype(jnp.float32),
        lax.psum(grad_b_down.astype(jnp.bfloat16), "dp").astype(jnp.float32),
        lax.psum(grad_w_ada.astype(jnp.bfloat16), "dp").astype(jnp.float32),
        lax.psum(grad_b_ada.astype(jnp.bfloat16), "dp").astype(jnp.float32),
    )
    return (
        output,
        grad_tokens,
        grad_condition,
        grad_w_qkv,
        grad_qv_bias,
        grad_w_out,
        grad_b_out,
        grad_w_up,
        grad_b_up,
        grad_w_down,
        grad_b_down,
        grad_w_ada,
        grad_b_ada,
    )


def solution(mesh):
    return jax.shard_map(
        shards,
        mesh=mesh,
        in_specs=(
            P(("dp", "mp"), None),
            P("dp", None),
            P("dp"),
            P("dp"),
            P("dp"),
            P("dp"),
            P("dp"),
            P(None, None, "mp"),
            P(None, "mp"),
            P("mp", None),
            P(),
            P(None, "mp"),
            P("mp"),
            P("mp", None),
            P(),
            P(None, None, "mp"),
            P(None, "mp"),
            P(("dp", "mp"), None),
        ),
        out_specs=(
            P(("dp", "mp"), None),
            P(("dp", "mp"), None),
            P("dp", None),
            P(None, None, "mp"),
            P(None, "mp"),
            P("mp", None),
            P(),
            P(None, "mp"),
            P("mp"),
            P("mp", None),
            P(),
            P(None, None, "mp"),
            P(None, "mp"),
        ),
        check_vma=False,
    )
```

profile of v0, /device:TPU:0, one launch (start us, length us, event | category | flops | bytes accessed | tf_op | source)
XLA Modules:
  0.0 1440.0 jit_solution(4666563923387932333)
XLA Ops:
  16.8 12.6 all_gather.15
  31.3 14.9 %fusion.77 = f32[1024,6,1152]{2,0,1:T(8,128)} fusion(s32[1024]{0:T(1024)S(1)} %dynamic_slice.3, f32[1,2,6,1152]{3,2,1,0:T(8,128)S(1)} %bitcast.233), kind=kOutput, calls=%fused_computation.121 | convolution fusion | flops 169871360 | bytes 28370944 | tf_op jit(solution)/shard_map/dot_general | solution.py:101
  46.2 5.4 fusion.28
  55.3 61.7 %all-gather.5.cloned.1.call-done = bf16[4096,1152]{1,0:T(8,128)(2,1)} async-done(((bf16[1024,1152]{1,0:T(8,128)(2,1)}), bf16[4096,1152]{1,0:T(8,128)(2,1)}) %all-gather.5.cloned.1.call-update) | async-done | bytes 9437200 | tf_op jit(solution)/shard_map/all_gather | solution.py:108
  117.0 12.5 add_convert_fusion
  136.4 19.2 %fusion.104 = (f32[8,4,512]{2,1,0:T(4,128)S(1)}, f32[8,4,512,512]{2,3,1,0:T(8,128)}) fusion(bf16[8,512,4,72]{1,0,3,2:T(8,128)(2,1)S(1)} %bitcast.212, bf16[8,512,4,72]{1,0,3,2:T(8,128)(2,1)} %bitcast.221, pred[8,512,512]{1,2,0:T(8,128)(4,1)} %and_or_fusion), kind=kOutput, calls=%fused_computation.164 | convolution fusion | flops 1233108992 | bytes 40435712 | tf_op jit(solution)/shard_map/bqhe,bkhe->bhqk/dot_general | solution.py:129
  155.6 13.1 fusion
  168.8 16.2 %convert_bitcast_fusion.2 = bf16[8,512,4,72]{1,3,2,0:T(8,128)(2,1)} fusion(f32[8,4,512,512]{2,3,1,0:T(8,128)} %get-tuple-element.46, f32[8,4,512]{2,1,0:T(4,128)S(1)} %fusion, f32[8,4,512]{2,1,0:T(4,128)S(1)} %get-tuple-element.45, bf16[8,512,4,72]{1,0,3,2:T(8,128)(2,1)} %bitcast.214), kind=kOutput, calls=%fused_computation.94 | convolution fusion | flops 1234305024 | bytes 38404096 | tf_op jit(solution)/shard_map/bhqk,bkhe->bqhe/dot_general | solution.py:139
  190.6 8.0 convolution_convert_fusion.2
  199.3 77.9 %reduce-scatter.8.cloned.1.call-done = bf16[1024,1152]{1,0:T(8,128)(2,1)} async-done(((bf16[4096,1152]{1,0:T(8,128)(2,1)}), bf16[1024,1152]{1,0:T(8,128)(2,1)}) %reduce-scatter.8.cloned.1.call-update) | async-done | bytes 2359312 | tf_op jit(solution)/shard_map/reduce_scatter | solution.py:141
  277.2 4.8 fusion.100
  285.3 8.0 fusion.31
  294.0 63.8 %all-gather.9.cloned.1.call-done = bf16[4096,1152]{1,0:T(8,128)(2,1)} async-done(((bf16[1024,1152]{1,0:T(8,128)(2,1)}), bf16[4096,1152]{1,0:T(8,128)(2,1)}) %all-gather.9.cloned.1.call-update) | async-done | bytes 9437200 | tf_op jit(solution)/shard_map/all_gather | solution.py:164
  357.7 19.7 %fusion.107 = f32[4096,1152]{1,0:T(8,128)} fusion(bf16[4096,1152]{1,0:T(8,128)(2,1)} %all-gather.9.cloned.1.call-done, bf16[1152,1152]{1,0:T(8,128)(2,1)} %param.31), kind=kOutput, calls=%fused_computation.167 | convolution fusion | flops 10871635968 | bytes 30965760 | tf_op jit(solution)/shard_map/dot_general | solution.py:48
  377.5 46.5 %all-gather.7.cloned.1.call-done = bf16[4096,1152]{1,0:T(8,128)(2,1)} async-done(((bf16[1024,1152]{1,0:T(8,128)(2,1)}), bf16[4096,1152]{1,0:T(8,128)(2,1)}) %all-gather.7.cloned.1.call-update) | async-done | bytes 9437200 | tf_op jit(solution)/shard_map/all_gather | solution.py:149
  424.0 30.1 %fusion.95 = (bf16[1152]{0:T(1024)(128)(2,1)}, bf16[4096,1152]{1,0:T(8,128)(2,1)S(1)}, f32[4096,1152]{1,0:T(8,128)}) fusion(f32[4096,1152]{1,0:T(8,128)} %fusion.107, f32[1152]{0:T(1024)S(1)} %convert_element_type.196, bf16[4096,1152]{1,0:T(8,128)(2,1)} %all-gather.7.cloned.1.call-done, bf16[1152,1152]{1,0:T(8,128)(2,1)S(1)} %copy-done), kind=kOutput, calls=%fused_computation.156 | convolution fusion | flops 10975443968 | bytes 59284224 | tf_op jit(solution)/shard_map/dot_general | solution.py:150
  457.7 15.9 %convolution_convert_fusion = bf16[4096,1152]{1,0:T(8,128)(2,1)} fusion(bf16[4096,1152]{1,0:T(8,128)(2,1)S(1)} %get-tuple-element.26, bf16[1152,1152]{1,0:T(8,128)(2,1)S(1)} %copy-done), kind=kOutput, calls=%fused_computation.25 | convolution fusion | flops 10876354560 | bytes 21528576 | tf_op jit(solution)/shard_map/dot_general | solution.py:48
  475.4 22.5 %convolution_convert_fusion.1 = bf16[4096,1152]{1,0:T(8,128)(2,1)} fusion(bf16[1152,1152]{1,0:T(8,128)(2,1)S(1)} %copy-done.59, f32[4096,1152]{1,0:T(8,128)} %get-tuple-element.47), kind=kOutput, calls=%fused_computation.26 | convolution fusion | flops 10918821888 | bytes 30965760 | tf_op jit(solution)/shard_map/dot_general | solution.py:155
  498.6 53.6 %reduce-scatter.12.cloned.1.call-done = bf16[1024,1152]{1,0:T(8,128)(2,1)} async-done(((bf16[4096,1152]{1,0:T(8,128)(2,1)}), bf16[1024,1152]{1,0:T(8,128)(2,1)}) %reduce-scatter.12.cloned.1.call-update) | async-done | bytes 2359312 | tf_op jit(solution)/shard_map/reduce_scatter | solution.py:172
  552.3 5.5 multiply_reduce_fusion.1
  557.7 75.4 %reduce-scatter.10.cloned.1.call-done = bf16[1024,1152]{1,0:T(8,128)(2,1)} async-done(((bf16[4096,1152]{1,0:T(8,128)(2,1)}), bf16[1024,1152]{1,0:T(8,128)(2,1)}) %reduce-scatter.10.cloned.1.call-update) | async-done | bytes 2359312 | tf_op jit(solution)/shard_map/reduce_scatter | solution.py:154
  633.2 9.2 fusion.99
  644.6 4.7 multiply_convert_fusion.2
  649.5 64.3 %all-gather.11.cloned.1.call-done = bf16[4096,1152]{1,0:T(8,128)(2,1)} async-done(((bf16[1024,1152]{1,0:T(8,128)(2,1)}), bf16[4096,1152]{1,0:T(8,128)(2,1)}) %all-gather.11.cloned.1.call-update) | async-done | bytes 9437200 | tf_op jit(solution)/shard_map/all_gather | solution.py:180
  713.8 10.0 convolution_convert_fusion.5
  724.9 15.2 %fusion.49 = bf16[8,512,4,72]{1,3,2,0:T(8,128)(2,1)} fusion(f32[8,4,512,512]{2,3,1,0:T(8,128)} %get-tuple-element.46, f32[8,4,512]{2,1,0:T(4,128)S(1)} %bitcast.230, bf16[8,512,4,72]{1,0,3,2:T(8,128)(2,1)S(1)} %bitcast.209), kind=kOutput, calls=%fused_computation.95 | convolution fusion | flops 1224736768 | bytes 38338560 | tf_op jit(solution)/shard_map/bhqk,bqhe->bkhe/dot_general | solution.py:188
  740.1 26.8 %multiply_reduce_fusion = (f32[8,4,512]{2,1,0:T(4,128)S(1)}, f32[8,4,512,512]{2,3,1,0:T(8,128)}) fusion(f32[8,4,512,512]{2,3,1,0:T(8,128)} %get-tuple-element.46, f32[8,4,512]{2,1,0:T(4,128)S(1)} %bitcast.231, bf16[8,512,4,72]{1,0,3,2:T(8,128)(2,1)} %bitcast.215, bf16[8,512,4,72]{1,0,3,2:T(8,128)(2,1)S(1)} %bitcast.210), kind=kOutput, calls=%fused_computation.1 | convolution fusion | flops 1233108992 | bytes 71958528 | tf_op jit(solution)/shard_map/bqhe,bkhe->bhqk/dot_general | solution.py:185
  766.9 27.6 %multiply_convert_fusion = bf16[8,4,512,512]{2,3,1,0:T(8,128)(2,1)} fusion(f32[8,4,512,512]{2,3,1,0:T(8,128)} %get-tuple-element.49, f32[8,4,512,512]{2,3,1,0:T(8,128)} %get-tuple-element.46, f32[8,4,512]{2,1,0:T(4,128)S(1)} %get-tuple-element.48, f32[8,4,512]{2,1,0:T(4,128)S(1)} %bitcast.232), kind=kLoop, calls=%fused_computation | loop fusion | flops 33554432 | bytes 84017152 | tf_op jit(solution)/shard_map/convert_element_type | solution.py:195
  794.5 10.9 multiply_bitcast_fusion
  805.3 10.3 multiply_bitcast_fusion.1
  818.4 5.1 stack_reshape.11
  826.2 5.0 stack_reshape.9
  843.9 13.3 bitcast_convert_fusion
  857.4 18.6 %convolution_convert_fusion.4 = bf16[1152,1152]{1,0:T(8,128)(2,1)} fusion(bf16[4096,1152]{1,0:T(8,128)(2,1)} %all-gather.7.cloned.1.call-done, bf16[4096,1152]{1,0:T(8,128)(2,1)} %copy-done.63), kind=kOutput, calls=%fused_computation.36 | convolution fusion | flops 10872963072 | bytes 21528576 | tf_op jit(solution)/shard_map/dot_general | solution.py:42
  876.0 20.3 %convolution_convert_fusion.3 = bf16[1152,1152]{1,0:T(8,128)(2,1)} fusion(bf16[4096,1152]{1,0:T(8,128)(2,1)} %all-gather.9.cloned.1.call-done, f32[4096,1152]{1,0:T(8,128)} %get-tuple-element.47), kind=kOutput, calls=%fused_computation.35 | convolution fusion | flops 10915430400 | bytes 30965760 | tf_op jit(solution)/shard_map/dot_general | solution.py:42
  896.3 10.6 fusion.44
  907.0 28.9 %reduce-scatter.14.cloned.1.call-done = bf16[1024,1152]{1,0:T(8,128)(2,1)} async-done(((bf16[4096,1152]{1,0:T(8,128)(2,1)}), bf16[1024,1152]{1,0:T(8,128)(2,1)}) %reduce-scatter.14.cloned.1.call-update) | async-done | bytes 2359312 | tf_op jit(solution)/shard_map/reduce_scatter | solution.py:216
  943.8 6.8 bitcast_dynamic-update-slice_fusion
  958.8 27.7 %copy.101 = f32[1024,6,1152]{0,2,1:T(8,128)} copy(f32[1024,6,1152]{2,0,1:T(8,128)} %fusion.33) | data formatting | bytes 56623104 | tf_op jit(solution)/shard_map/stack | solution.py:222
  986.5 16.0 %fusion.52 = bf16[2,6,1152]{2,0,1:T(2,128)(2,1)S(1)} fusion(f32[1024,6,1152]{0,2,1:T(8,128)} %copy.101, s32[1024]{0:T(1024)S(1)} %copy-done.46), kind=kOutput, calls=%fused_computation.96 | convolution fusion | flops 169885184 | bytes 28343296 | tf_op jit(solution)/shard_map/dot_general | solution.py:233
  1009.2 8.4 convolution_convert_fusion.7
  1017.6 11.7 reduce-scatter.16.cloned.1.call-done
  1034.4 5.0 reduce_sum.212
  1039.4 5.9 reduce_sum.210
  1045.4 4.4 fusion.30
  1057.1 39.4 %all-reduce = (bf16[2,288]{1,0:T(2,128)(2,1)S(1)}, bf16[1152]{0:T(1024)(128)(2,1)S(1)}, bf16[1152]{0:T(1024)(128)(2,1)S(1)}, bf16[1152]{0:T(1024)(128)(2,1)S(1)}, bf16[6,288]{1,0:T(8,128)(2,1)S(1)}) all-reduce(bf16[2,288]{1,0:T(2,128)(2,1)S(1)} %pad_maximum_fusion, ...), channel_id=1, replica_groups=mesh['dp'=8,'mp'=4] {'dp'}, use_global_device_ids=true, to_apply=%region_21.22 | all-reduce | flops 5760 | bytes 23040 | tf_op jit(solution)/shard_map/psum | solution.py:263
  1102.3 6.3 psum.77
  1109.2 307.3 %all-reduce.4.cloned.1.call-done = (bf16[1152,3,288]{0,2,1:T(8,128)(2,1)}, bf16[288,1152]{1,0:T(8,128)(2,1)}, bf16[1152,1152]{1,0:T(8,128)(2,1)}, bf16[1152,1152]{1,0:T(8,128)(2,1)}, bf16[1152,6,288]{0,2,1:T(8,128)(2,1)}) async-done(((bf16[1152,3,288]{0,2,1:T(8,128)(2,1)}, bf16[288,1152]{1,0:T(8,128)(2,1)}, bf16[1152,1152]{1,0:T(8,128)(2,1)}, bf16[1152,1152]{1,0:T(8,128)(2,1)}, ...) | async-done | bytes 11943952 | tf_op jit(solution)/shard_map/psum | solution.py:262
  (244 shorter events, 116.7 us)
Async XLA Ops:
  7.2 416.8 %copy-start = (bf16[1152,1152]{1,0:T(8,128)(2,1)S(1)}, bf16[1152,1152]{1,0:T(8,128)(2,1)}, u32[]{:S(2)}) copy-start(bf16[1152,1152]{1,0:T(8,128)(2,1)} %param.29) | copy-start | bytes 7962628
  7.2 109.7 %all-gather.5.cloned.1.call-start = ((), (), s32[]{:S(2)}) async-start(), calls=%async_computation.5 | async-start | bytes 11796480 | tf_op jit(solution)/shard_map/all_gather | solution.py:108
  10.1 36.1 %copy-start.31 = (f32[1024]{0:T(1024)}, f32[1024]{0:T(1024)S(1)}, u32[]{:S(2)}) copy-start(f32[1024]{0:T(1024)S(1)} %broadcast_multiply_fusion.1) | copy-start | bytes 12292
  10.1 20.9 %copy-start.55 = (s32[16]{0:T(128)S(1)}, s32[16]{0:T(128)}, u32[]{:S(2)}) copy-start(s32[16]{0:T(128)} %param.22) | copy-start | bytes 196
  10.2 20.9 %copy-start.57 = (s32[16]{0:T(128)S(1)}, s32[16]{0:T(128)}, u32[]{:S(2)}) copy-start(s32[16]{0:T(128)} %param.20) | copy-start | bytes 196
  10.2 20.9 %copy-start.58 = (s32[16]{0:T(128)S(1)}, s32[16]{0:T(128)}, u32[]{:S(2)}) copy-start(s32[16]{0:T(128)} %param.21) | copy-start | bytes 196
  10.2 20.9 %copy-start.56 = (s32[16]{0:T(128)S(1)}, s32[16]{0:T(128)}, u32[]{:S(2)}) copy-start(s32[16]{0:T(128)} %param.23) | copy-start | bytes 196
  12.7 33.5 %copy-start.39 = (f32[1024]{0:T(1024)}, f32[1024]{0:T(1024)S(1)}, u32[]{:S(2)}) copy-start(f32[1024]{0:T(1024)S(1)} %fusion.89) | copy-start | bytes 12292
  31.3 14.9 %copy-start.45 = (s32[1024]{0:T(1024)}, s32[1024]{0:T(1024)S(1)}, u32[]{:S(2)}) copy-start(s32[1024]{0:T(1024)S(1)} %dynamic_slice.3) | copy-start | bytes 12292
  31.3 14.9 %copy-start.3 = (bf16[1024,1152]{1,0:T(8,128)(2,1)S(1)}, bf16[1024,1152]{1,0:T(8,128)(2,1)}, u32[]{:S(2)}) copy-start(bf16[1024,1152]{1,0:T(8,128)(2,1)} %param.18) | copy-start | bytes 7077892
  51.7 225.5 %reduce-scatter.8.cloned.1.call-start = ((), (), s32[]{:S(2)}) async-start(), calls=%async_computation.6 | async-start | bytes 11796480 | tf_op jit(solution)/shard_map/reduce_scatter | solution.py:141
  133.9 21.6 %copy-start.14 = (bf16[36,8,8,512]{3,2,1,0:T(8,128)(2,1)}, bf16[36,8,8,512]{3,2,1,0:T(8,128)(2,1)S(1)}, u32[]{:S(2)}) copy-start(bf16[36,8,8,512]{3,2,1,0:T(8,128)(2,1)S(1)} %copy.115) | copy-start | bytes 7077892
  155.6 13.2 copy-start.25
  168.8 16.2 %copy-start.27 = (f32[8,4,512]{2,1,0:T(4,128)}, f32[8,4,512]{2,1,0:T(4,128)S(1)}, u32[]{:S(2)}) copy-start(f32[8,4,512]{2,1,0:T(4,128)S(1)} %fusion) | copy-start | bytes 196612
  198.6 159.1 %all-gather.9.cloned.1.call-start = ((), (), s32[]{:S(2)}) async-start(), calls=%async_computation.9 | async-start | bytes 11796480 | tf_op jit(solution)/shard_map/all_gather | solution.py:164
  199.3 82.7 %copy-start.33 = (f32[1152]{0:T(1024)}, f32[1152]{0:T(1024)S(1)}, u32[]{:S(2)}) copy-start(f32[1152]{0:T(1024)S(1)} %convert_element_type.194) | copy-start | bytes 13828
  281.9 11.4 copy-start.2
  282.0 351.2 %copy-start.29 = (f32[1024]{0:T(1024)}, f32[1024]{0:T(1024)S(1)}, u32[]{:S(2)}) copy-start(f32[1024]{0:T(1024)S(1)} %broadcast_multiply_fusion) | copy-start | bytes 12292
  285.3 347.9 %copy-start.37 = (f32[1024]{0:T(1024)}, f32[1024]{0:T(1024)S(1)}, u32[]{:S(2)}) copy-start(f32[1024]{0:T(1024)S(1)} %fusion.90) | copy-start | bytes 12292
  293.3 130.7 %all-gather.7.cloned.1.call-start = ((), (), s32[]{:S(2)}) async-start(), calls=%async_computation.7 | async-start | bytes 11796480 | tf_op jit(solution)/shard_map/all_gather | solution.py:149
  293.9 258.3 %reduce-scatter.12.cloned.1.call-start = ((), (), s32[]{:S(2)}) async-start(), calls=%async_computation.10 | async-start | bytes 11796480 | tf_op jit(solution)/shard_map/reduce_scatter | solution.py:172
  473.7 159.5 %reduce-scatter.10.cloned.1.call-start = ((), (), s32[]{:S(2)}) async-start(), calls=%async_computation.8 | async-start | bytes 11796480 | tf_op jit(solution)/shard_map/reduce_scatter | solution.py:154
  497.9 215.9 %all-gather.11.cloned.1.call-start = ((), (), s32[]{:S(2)}) async-start(), calls=%async_computation.11 | async-start | bytes 11796480 | tf_op jit(solution)/shard_map/all_gather | solution.py:180
  498.6 134.6 %copy-start.35 = (f32[1152]{0:T(1024)}, f32[1152]{0:T(1024)S(1)}, u32[]{:S(2)}) copy-start(f32[1152]{0:T(1024)S(1)} %convert_element_type.200) | copy-start | bytes 13828
  557.7 86.9 %copy-start.7 = (bf16[1024,1152]{1,0:T(8,128)(2,1)S(1)}, bf16[1024,1152]{1,0:T(8,128)(2,1)}, u32[]{:S(2)}) copy-start(bf16[1024,1152]{1,0:T(8,128)(2,1)} %param.35) | copy-start | bytes 7077892
  642.4 6.9 copy-start.41
  644.6 69.2 %copy-start.62 = (bf16[288,1152]{1,0:T(8,128)(2,1)S(1)}, bf16[288,1152]{1,0:T(8,128)(2,1)}, u32[]{:S(2)}) copy-start(bf16[288,1152]{1,0:T(8,128)(2,1)} %param.27) | copy-start | bytes 1990660
  649.4 286.5 %reduce-scatter.14.cloned.1.call-start = ((), (), s32[]{:S(2)}) async-start(), calls=%async_computation.12 | async-start | bytes 11796480 | tf_op jit(solution)/shard_map/reduce_scatter | solution.py:216
  766.9 27.6 %copy-start.18 = (bf16[36,8,8,512]{3,2,1,0:T(8,128)(2,1)S(1)}, bf16[36,8,8,512]{3,2,1,0:T(8,128)(2,1)}, u32[]{:S(2)}) copy-start(bf16[36,8,8,512]{3,2,1,0:T(8,128)(2,1)} %copy.114) | copy-start | bytes 7077892
  794.5 10.9 copy-start.15
  805.3 10.3 copy-start.13
  836.7 7.3 copy-start.60
  857.3 172.1 %reduce-scatter.16.cloned.1.call-start = ((), (), s32[]{:S(2)}) async-start(), calls=%async_computation.13 | async-start | bytes 368640
  857.3 39.0 %slice-start.4 = ((s8[7077888]{0:T(1024)(128)(4,1)}), s8[4194304]{0:T(1024)(128)(4,1)S(1)}, s32[]{:S(2)}) async-start(s8[7077888]{0:T(1024)(128)(4,1)} %bitcast.225), calls=%async_computation.19 | async-start | bytes 8388608
  857.3 39.0 %slice-start.6 = ((s8[9437184]{0:T(1024)(128)(4,1)}), s8[4194304]{0:T(1024)(128)(4,1)S(1)}, s32[]{:S(2)}) async-start(s8[9437184]{0:T(1024)(128)(4,1)} %bitcast.237), calls=%async_computation.21 | async-start | bytes 8388608
  857.3 39.0 %slice-start.7 = ((s8[9437184]{0:T(1024)(128)(4,1)}), s8[4194304]{0:T(1024)(128)(4,1)S(1)}, s32[]{:S(2)}) async-start(s8[9437184]{0:T(1024)(128)(4,1)} %bitcast.237), calls=%async_computation.22 | async-start | bytes 8388608
  876.0 20.3 %slice-start.5 = ((s8[7077888]{0:T(1024)(128)(4,1)}), s8[2883584]{0:T(1024)(128)(4,1)S(1)}, s32[]{:S(2)}) async-start(s8[7077888]{0:T(1024)(128)(4,1)} %bitcast.225), calls=%async_computation.20 | async-start | bytes 5767168
  876.0 20.3 %slice-start.8 = ((s8[9437184]{0:T(1024)(128)(4,1)}), s8[1048576]{0:T(1024)(128)(4,1)S(1)}, s32[]{:S(2)}) async-start(s8[9437184]{0:T(1024)(128)(4,1)} %bitcast.237), calls=%async_computation.23 | async-start | bytes 2097152
  907.0 33.1 %copy-start.4 = (bf16[1024,1152]{1,0:T(8,128)(2,1)S(1)}, bf16[1024,1152]{1,0:T(8,128)(2,1)}, u32[]{:S(2)}) copy-start(bf16[1024,1152]{1,0:T(8,128)(2,1)} %param.18) | copy-start | bytes 7077892
  907.0 33.1 %copy-start.32 = (f32[1024]{0:T(1024)S(1)}, f32[1024]{0:T(1024)}, u32[]{:S(2)}) copy-start(f32[1024]{0:T(1024)} %copy-done.31) | copy-start | bytes 12292
  907.0 33.1 %copy-start.40 = (f32[1024]{0:T(1024)S(1)}, f32[1024]{0:T(1024)}, u32[]{:S(2)}) copy-start(f32[1024]{0:T(1024)} %copy-done.39) | copy-start | bytes 12292
  940.2 12.9 slice-start
  943.8 6.9 copy-start.10
  943.8 9.3 slice-start.1
  958.7 27.7 %copy-start.46 = (s32[1024]{0:T(1024)S(1)}, s32[1024]{0:T(1024)}, u32[]{:S(2)}) copy-start(s32[1024]{0:T(1024)} %copy-done.45) | copy-start | bytes 12292
  1008.9 22.3 %copy-start.44 = (bf16[2,1152]{1,0:T(2,128)(2,1)S(1)}, bf16[2,1152]{1,0:T(2,128)(2,1)}, u32[]{:S(2)}) copy-start(bf16[2,1152]{1,0:T(2,128)(2,1)} %param.19) | copy-start | bytes 13828
  1008.9 407.6 %all-reduce.4.cloned.1.call-start = ((), (), s32[]{:S(2)}) async-start(), calls=%async_computation.14 | async-start | bytes 23887872 | tf_op jit(solution)/shard_map/psum | solution.py:262
  1045.4 8.6 slice-start.2
  (35 other events, 122.6 us)
Sparse Core Ops, SparseCore 0:
  51.8 65.1 all-gather.4
  198.7 78.3 reduce-scatter.7
  293.4 64.2 all-gather.8
  359.7 64.2 all-gather.6
  473.8 78.4 reduce-scatter.11
  554.7 78.4 reduce-scatter.9
  649.5 64.2 all-gather.10
  857.4 78.4 reduce-scatter.13
  1009.0 20.2 reduce-scatter.15
  1036.3 380.1 all-reduce.3
where the time goes:
time: 1450 us; the launch traced here: 1440 us
  waiting for transfers between devices  792 us (55%)
  matrix products  329 us (23%)
  other arithmetic  155 us (11%)
  local copies, waits for them, and re-layouts  89.2 us (6%)
  blocking collectives  58.3 us (4%)
  between operations  16 us (1%)
    psum x1, waiting for transfers between devices, shards(): lax.psum(grad_w_qkv.astype(jnp.bfloat16), 'dp').astype(jnp.float32)  307 us
    reduce_scatter x1, waiting for transfers between devices, shards(): lax.psum_scatter(jnp.dot(attended, w_out, preferred_element_type=jnp.floa...  77.9 us
    reduce_scatter x1, waiting for transfers between devices, shards(): lax.psum_scatter(jnp.dot(hidden, w_down, preferred_element_type=jnp.float...  75.4 us
    all_gather x1, waiting for transfers between devices, shards(): full_one = lax.all_gather(grad_branch_one, 'mp', axis=0, tiled=True)  64.3 us
    all_gather x1, waiting for transfers between devices, shards(): full_two = lax.all_gather(grad_branch_two, 'mp', axis=0, tiled=True)  63.8 us
    all_gather x1, waiting for transfers between devices, shards(): gathered_one = lax.all_gather(normed_one, 'mp', axis=0, tiled=True)  61.7 us
    dot_general x4, matrix products, col_inner(): lax.dot_general(left, right, (((1,), (1,)), ((), ())), preferred_element_...  59 us
    dot_general x4, matrix products, row_inner(): lax.dot_general(left, right, (((0,), (0,)), ((), ())), preferred_element_...  58 us
  transfers between devices with their start and end apart: 10, of which 10 were waited for; matrix products, arithmetic and copies ran while one was open for 10% of the time, Pallas kernels for 0%

commit v1 on v0

v1 whole, which is shorter than its diff:
```python
import functools

import jax
import jax.numpy as jnp
from jax import lax
from jax.experimental import pallas as pl
from jax.experimental.pallas import tpu as pltpu
from jax.sharding import PartitionSpec as P

HEAD = 72
SLOT = 256
CHUNK = 128
OUT_SLOTS = 6
MESH = pl.DeviceIdType.MESH
epsilon = 1e-06
f32 = jnp.float32
bf16 = jnp.bfloat16


def frame_tables(grid_rows, grid_cols, frame_start, frame_item, used, first, length):
    rows = first + jnp.arange(length, dtype=jnp.int32)[:, None]
    slots = jnp.arange(grid_rows.shape[0], dtype=jnp.int32)[None, :]
    ends = (frame_start + grid_rows * grid_cols)[None, :]
    inside = (rows >= frame_start[None, :]) & (rows < ends) & (slots < used)
    frame_id = jnp.sum(jnp.where(inside, slots + 1, 0), axis=1) - 1
    item_id = jnp.sum(jnp.where(inside, frame_item[None, :], 0), axis=1)
    return (frame_id, item_id)


def normal(values):
    centred = values - jnp.mean(values, axis=-1, keepdims=True)
    rstd = lax.rsqrt(jnp.mean(centred * centred, axis=-1, keepdims=True) + epsilon)
    return centred * rstd, rstd


def normal_back(grad, scale, normed, rstd):
    u = grad * (1.0 + scale)
    return rstd * (
        u
        - jnp.mean(u, axis=-1, keepdims=True)
        - normed * jnp.mean(u * normed, axis=-1, keepdims=True)
    )


def dot(left, right):
    return jnp.dot(left, right, preferred_element_type=f32)


def row_inner(left, right):
    return lax.dot_general(left, right, (((0,), (0,)), ((), ())), preferred_element_type=f32)


def col_inner(left, right):
    return lax.dot_general(left, right, (((1,), (1,)), ((), ())), preferred_element_type=f32)


def reduce_kernel(count, g_ref, out_ref, lp, rd, s0, sx, rx, tb, ry, ub, rz1, vb, rz2, ob, loads, sends, recvs, outs):
    dp, mp = lax.axis_index("dp"), lax.axis_index("mp")
    core, yb = mp % 2, dp % 2
    xb, z0, z1 = mp // 2, (dp // 2) % 2, dp // 4
    sib = (dp, mp + 1 - 2 * core)
    xn = (dp, mp + 2 - 4 * xb)
    yn = (dp + 1 - 2 * yb, mp)
    z1n = (dp + 2 - 4 * z0, mp)
    z2n = (dp + 4 - 8 * z1, mp)
    half, quarter, eighth = CHUNK // 2, CHUNK // 4, CHUNK // 8

    barrier = pltpu.get_barrier_semaphore()
    for peer in (sib, xn, yn, z1n, z2n):
        pl.semaphore_signal(barrier, inc=1, device_id=peer, device_id_type=MESH)
    pl.semaphore_wait(barrier, 5)

    def rows_of(c):
        return pl.ds(pl.multiple_of(c * CHUNK, CHUNK), CHUNK)

    def remote(stage, src, dst, peer, slot):
        return pltpu.make_async_remote_copy(
            src_ref=src,
            dst_ref=dst,
            send_sem=sends.at[stage, slot],
            recv_sem=recvs.at[stage, slot],
            device_id=peer,
            device_id_type=MESH,
        )

    def load(which, c, slot):
        return pltpu.make_async_copy(
            g_ref.at[2 * which, rows_of(c)], lp.at[slot, which], loads.at[which, slot]
        )

    def d_copy(which, c, slot):
        return remote(which, g_ref.at[2 * which + 1, rows_of(c)], rd.at[slot, which], sib, slot)

    def x_copy(c, slot):
        return remote(2, sx.at[slot], rx.at[slot], xn, slot)

    def y_copy(c, slot):
        part = pl.ds(pl.multiple_of((1 - yb) * half, half), half)
        return remote(3, tb.at[slot, part], ry.at[slot], yn, slot)

    def z1_copy(c, slot):
        part = pl.ds(pl.multiple_of((1 - z0) * quarter, quarter), quarter)
        return remote(4, ub.at[slot, part], rz1.at[slot], z1n, slot)

    def z2_copy(c, slot):
        part = pl.ds(pl.multiple_of((1 - z1) * eighth, eighth), eighth)
        return remote(5, vb.at[slot, part], rz2.at[slot], z2n, slot)

    at_y = pl.multiple_of(yb * half, half)
    at_z1 = pl.multiple_of(yb * half + z0 * quarter, quarter)
    at_z2 = pl.multiple_of(yb * half + z0 * quarter + z1 * eighth, eighth)

    def back(stage, at, size, peer, c, slot):
        place = ob.at[c % OUT_SLOTS, pl.ds(at, size)]
        return remote(stage, place, place, peer, slot)

    def az2_copy(c, slot):
        return back(6, at_z2, eighth, z2n, c, slot)

    def az1_copy(c, slot):
        return back(7, at_z1, quarter, z1n, c, slot)

    def ay_copy(c, slot):
        return back(8, at_y, half, yn, c, slot)

    def out_copy(c, slot):
        return pltpu.make_async_copy(ob.at[c % OUT_SLOTS], out_ref.at[rows_of(c)], outs.at[slot])

    def step(i, carry):
        def stage(lag, work):
            c = i - lag

            @pl.when((c >= 0) & (c < count))
            def _():
                work(c, c % 2)

        def leave(c, slot):
            out_copy(c, slot).wait()

        def store(c, slot):
            ay_copy(c, slot).wait()
            out_copy(c, slot).start()

        def go_ay(c, slot):
            az1_copy(c, slot).wait()
            ay_copy(c, slot).start()

        def go_az1(c, slot):
            az2_copy(c, slot).wait()
            az1_copy(c, slot).start()

        def go_az2(c, slot):
            z2_copy(c, slot).wait()
            mine = vb[slot, pl.ds(pl.multiple_of(z1 * eighth, eighth), eighth)] + rz2[slot]
            ob[c % OUT_SLOTS, pl.ds(at_z2, eighth)] = mine
            az2_copy(c, slot).start()

        def go_z2(c, slot):
            z1_copy(c, slot).wait()
            vb[slot] = ub[slot, pl.ds(pl.multiple_of(z0 * quarter, quarter), quarter)] + rz1[slot]
            z2_copy(c, slot).start()

        def go_z1(c, slot):
            y_copy(c, slot).wait()
            ub[slot] = tb[slot, pl.ds(pl.multiple_of(yb * half, half), half)] + ry[slot]
            z1_copy(c, slot).start()

        def go_y(c, slot):
            x_copy(c, slot).wait()
            tb[slot] = s0[slot] + rx[slot]
            y_copy(c, slot).start()

        def go_x(c, slot):
            for which in range(2):
                load(which, c, slot).wait()
                d_copy(which, c, slot).wait()
            sx[slot] = lp[slot, 1] + rd[slot, 1]
            s0[slot] = lp[slot, 0] + rd[slot, 0]
            x_copy(c, slot).start()

        def go_d(c, slot):
            for which in range(2):
                load(which, c, slot).start()
                d_copy(which, c, slot).start()

        stage(9, leave)
        stage(8, store)
        stage(7, go_ay)
        stage(6, go_az1)
        stage(5, go_az2)
        stage(4, go_z2)
        stage(3, go_z1)
        stage(2, go_y)
        stage(1, go_x)
        stage(0, go_d)
        return carry

    lax.fori_loop(0, count + 10, step, 0)


def reduce_grads(parts):
    shards, rows, width = parts.shape
    count = rows // CHUNK
    half, quarter, eighth = CHUNK // 2, CHUNK // 4, CHUNK // 8

    def buf(*lead):
        return pltpu.VMEM((*lead, width), bf16)

    return pl.pallas_call(
        functools.partial(reduce_kernel, count),
        out_shape=jax.ShapeDtypeStruct((rows, width), bf16),
        in_specs=[pl.BlockSpec(memory_space=pl.ANY)],
        out_specs=pl.BlockSpec(memory_space=pl.ANY),
        scratch_shapes=[
            buf(2, 2, CHUNK),
            buf(2, 2, CHUNK),
            buf(2, CHUNK),
            buf(2, CHUNK),
            buf(2, CHUNK),
            buf(2, CHUNK),
            buf(2, half),
            buf(2, half),
            buf(2, quarter),
            buf(2, quarter),
            buf(2, eighth),
            buf(OUT_SLOTS, CHUNK),
            pltpu.SemaphoreType.DMA((2, 2)),
            pltpu.SemaphoreType.DMA((9, 2)),
            pltpu.SemaphoreType.DMA((9, 2)),
            pltpu.SemaphoreType.DMA((2,)),
        ],
        compiler_params=pltpu.CompilerParams(
            collective_id=0, has_side_effects=True, vmem_limit_bytes=32 << 20
        ),
    )(parts)


def swap(values, axis, bit):
    n = lax.axis_size(axis)
    return lax.ppermute(values, axis, [(i, i ^ bit) for i in range(n)])


def gather_weight(value):
    other = swap(value, "mp", 1)
    rows = value.shape[0] // 2
    side = lax.axis_index("dp") % 2
    mine = swap(lax.dynamic_slice_in_dim(value, side * rows, rows), "mp", 2)
    rest = swap(mine, "dp", 1)
    far = jnp.concatenate(
        [jnp.where(side == 0, mine, rest), jnp.where(side == 0, rest, mine)], axis=0
    )
    return [value, other, far, swap(far, "mp", 1)]


def shards(
    paired,
    tokens,
    condition,
    grid_rows,
    grid_cols,
    frame_start,
    frame_item,
    group_frames,
    w_qkv,
    qv_bias,
    w_out,
    b_out,
    w_up,
    b_up,
    w_down,
    b_down,
    w_ada,
    b_ada,
    cotangent,
):
    own_rows, width = tokens.shape
    local_width = w_qkv.shape[2]
    local_ff = w_up.shape[1]
    heads = local_width // HEAD
    items = condition.shape[0]
    n_mp, n_dp = lax.axis_size("mp"), lax.axis_size("dp")
    mp, dp = lax.axis_index("mp"), lax.axis_index("dp")
    frames = own_rows // SLOT
    scale = HEAD ** (-0.5)
    frame_id, item_id = frame_tables(
        grid_rows, grid_cols, frame_start, frame_item, group_frames[0], mp * own_rows, own_rows
    )
    cond_value = condition.astype(f32)
    act_low = jax.nn.silu(cond_value).astype(bf16)
    ada_flat = w_ada.reshape(width, -1)
    ada_local = dot(act_low, ada_flat) + b_ada.reshape(-1).astype(f32)
    bias_local = jnp.concatenate(
        [
            qv_bias[0].astype(f32),
            jnp.zeros((local_width,), f32),
            qv_bias[1].astype(f32),
            b_up.astype(f32),
        ]
    )
    small = jnp.concatenate([ada_local.reshape(-1), bias_local])
    small = lax.all_gather(small, "mp", axis=0)
    n_ada = items * 6 * local_width
    modulation = small[:, :n_ada].reshape(n_mp, items, 6, local_width)
    modulation = modulation.transpose(1, 2, 0, 3).reshape(items, 6, width)
    order = (mp ^ jnp.arange(n_mp)) if paired else jnp.arange(n_mp)
    biases = small[:, n_ada:][order]
    if paired:
        qkv = gather_weight(w_qkv.reshape(width, 3 * local_width))
        out = gather_weight(w_out)
        up = gather_weight(w_up)
        down = gather_weight(w_down)
    else:
        qkv = list(lax.all_gather(w_qkv.reshape(width, 3 * local_width), "mp", axis=0))
        out = list(lax.all_gather(w_out, "mp", axis=0))
        up = list(lax.all_gather(w_up, "mp", axis=0))
        down = list(lax.all_gather(w_down, "mp", axis=0))

    def per_row(k):
        total = modulation[0, k][None]
        for item in range(1, items):
            total = jnp.where((item_id == item)[:, None], modulation[item, k][None], total)
        return total

    inputs = tokens.astype(f32)
    upstream = cotangent.astype(f32)
    normed, rstd = normal(inputs)
    normed_one = (normed * (1.0 + per_row(1)) + per_row(0)).astype(bf16)
    ids = frame_id.reshape(frames, SLOT)
    place = jnp.arange(SLOT)
    allowed = ((ids[:, :, None] == ids[:, None, :]) & (ids[:, :, None] >= 0)) | (
        place[:, None] == place[None, :]
    )
    allowed = allowed[:, None]
    branch_one = b_out.astype(f32)[None]
    kept = []
    for m in range(n_mp):
        proj = (dot(normed_one, qkv[m]) + biases[m, : 3 * local_width][None]).astype(bf16)
        q, k, v = (
            proj[:, j * local_width : (j + 1) * local_width].reshape(frames, SLOT, heads, HEAD)
            for j in range(3)
        )
        scores = jnp.einsum("bqhe,bkhe->bhqk", q, k, preferred_element_type=f32) * scale
        scores = jnp.where(allowed, scores, -1e30)
        peak = jnp.max(scores, axis=-1, keepdims=True)
        weights = jnp.exp(scores - peak)
        totals = jnp.sum(weights, axis=-1, keepdims=True)
        probs = (weights / totals).astype(bf16)
        log_total = peak + jnp.log(totals)
        attended = jnp.einsum("bhqk,bkhe->bqhe", probs, v, preferred_element_type=f32)
        attended = attended.reshape(own_rows, local_width).astype(bf16)
        branch_one = branch_one + dot(attended, out[m])
        kept.append((q, k, v, log_total, attended))
    middle = inputs + per_row(2) * branch_one
    normed_mid, rstd_mid = normal(middle)
    normed_two = (normed_mid * (1.0 + per_row(4)) + per_row(3)).astype(bf16)
    gate_two = per_row(5)
    dbranch_two = (gate_two * upstream).astype(bf16)
    branch_two = b_down.astype(f32)[None]
    dnormed_two = jnp.zeros((own_rows, width), f32)
    g_up, g_down, g_attn, gb_up, gb_qv = [], [], [], [], []
    for m in range(n_mp):
        pre = dot(normed_two, up[m]) + biases[m, 3 * local_width :][None]
        hidden, pull = jax.vjp(lambda v: jax.nn.gelu(v, approximate=True), pre)
        hidden = hidden.astype(bf16)
        branch_two = branch_two + dot(hidden, down[m])
        dpre = pull(col_inner(dbranch_two, down[m]))[0].astype(bf16)
        g_down.append(row_inner(hidden, dbranch_two).astype(bf16))
        g_up.append(row_inner(normed_two, dpre).astype(bf16))
        gb_up.append(jnp.sum(dpre.astype(f32), axis=0))
        dnormed_two = dnormed_two + col_inner(dpre, up[m])
    output = (middle + gate_two * branch_two).astype(bf16)
    gb_down = jnp.sum(dbranch_two.astype(f32), axis=0)
    dmiddle = upstream + normal_back(dnormed_two, per_row(4), normed_mid, rstd_mid)
    dbranch_one = (per_row(2) * dmiddle).astype(bf16)
    gb_out = jnp.sum(dbranch_one.astype(f32), axis=0)
    dnormed_one = jnp.zeros((own_rows, width), f32)
    for m in range(n_mp):
        q, k, v, log_total, attended = kept[m]
        g_out = row_inner(attended, dbranch_one).astype(bf16)
        datt = col_inner(dbranch_one, out[m]).astype(bf16).reshape(frames, SLOT, heads, HEAD)
        scores = jnp.einsum("bqhe,bkhe->bhqk", q, k, preferred_element_type=f32) * scale
        probs = jnp.exp(jnp.where(allowed, scores, -1e30) - log_total)
        dprobs = jnp.einsum("bqhe,bkhe->bhqk", datt, v, preferred_element_type=f32)
        dv = jnp.einsum("bhqk,bqhe->bkhe", probs.astype(bf16), datt, preferred_element_type=f32)
        rowdot = jnp.sum(dprobs * probs, axis=-1, keepdims=True)
        dscores = (probs * (dprobs - rowdot)).astype(bf16)
        dq = jnp.einsum("bhqk,bkhe->bqhe", dscores, k, preferred_element_type=f32) * scale
        dk = jnp.einsum("bhqk,bqhe->bkhe", dscores, q, preferred_element_type=f32) * scale
        dproj = jnp.concatenate(
            [t.reshape(own_rows, local_width).astype(bf16) for t in (dq, dk, dv)], axis=1
        )
        sums = jnp.sum(dproj.astype(f32), axis=0)
        gb_qv.append(jnp.concatenate([sums[:local_width], sums[2 * local_width :]]))
        g_attn.append(jnp.concatenate([row_inner(dproj, normed_one).astype(bf16), g_out], axis=0))
        dnormed_one = dnormed_one + col_inner(dproj, qkv[m])
    grad_tokens = (dmiddle + normal_back(dnormed_one, per_row(1), normed, rstd)).astype(bf16)

    chosen = [(item_id == item)[:, None] for item in range(items)]

    def by_item(values):
        return jnp.stack([jnp.sum(jnp.where(c, values, 0.0), axis=0) for c in chosen])

    item_grad = jnp.stack(
        [
            by_item(dnormed_one),
            by_item(dnormed_one * normed),
            by_item(dmiddle * branch_one),
            by_item(dnormed_two),
            by_item(dnormed_two * normed_mid),
            by_item(upstream * branch_two),
        ],
        axis=1,
    )
    item_grad = item_grad.reshape(items, 6, n_mp, local_width).transpose(2, 0, 1, 3)[order]

    if paired:
        total_items = items * n_dp
        dmod_all = jnp.zeros((n_mp, total_items, 6, local_width), f32)
        dmod_all = lax.dynamic_update_slice(dmod_all, item_grad, (0, dp * items, 0, 0))
        act_all = jnp.zeros((total_items, width), f32)
        act_all = lax.dynamic_update_slice(act_all, act_low.astype(f32), (dp * items, 0))
        act_all = jnp.where(mp == 0, act_all, 0.0)
        fixed = jnp.concatenate([act_all, gb_out[None], gb_down[None]])
        n_dmod = total_items * 6 * local_width // width
        n_qv = -(-2 * local_width // width)
        tail = jnp.concatenate(
            [
                dmod_all.reshape(n_mp, n_dmod, width),
                jnp.broadcast_to(fixed[None], (n_mp, *fixed.shape)),
                jnp.stack(gb_up)[:, None],
                jnp.pad(jnp.stack(gb_qv), ((0, 0), (0, n_qv * width - 2 * local_width))).reshape(
                    n_mp, n_qv, width
                ),
            ],
            axis=1,
        )
        tail = jnp.pad(tail, ((0, 0), (0, -tail.shape[1] % CHUNK), (0, 0))).astype(bf16)
        parts = jnp.concatenate(
            [jnp.stack(g_up), jnp.stack(g_down), jnp.stack(g_attn), tail], axis=1
        )
        total = reduce_grads(parts)
        g_up, g_down = total[:width], total[width : 2 * width]
        g_attn, tail = total[2 * width : 3 * width], total[3 * width :].astype(f32)
        dmod = tail[:n_dmod].reshape(total_items, 6, local_width)
        at = n_dmod
        act_all = tail[at : at + total_items]
        at = at + total_items
        gb_out, gb_down, gb_up = tail[at], tail[at + 1], tail[at + 2]
        gb_qv = tail[at + 3 : at + 3 + n_qv].reshape(-1)[: 2 * local_width]
        own_dmod = lax.dynamic_slice_in_dim(dmod, dp * items, items)
    else:

        def over_mp(values):
            return lax.psum_scatter(values, "mp", scatter_dimension=0, tiled=False)

        def over_dp(values):
            return lax.psum(values.astype(bf16), "dp").astype(f32)

        own_dmod = over_mp(item_grad)
        dmod = lax.all_gather(own_dmod, "dp", axis=0, tiled=True)
        act_all = lax.all_gather(act_low, "dp", axis=0, tiled=True).astype(f32)
        g_up, g_down, g_attn = (
            over_dp(over_mp(jnp.stack(parts))) for parts in (g_up, g_down, g_attn)
        )
        gb_up = over_dp(over_mp(jnp.stack(gb_up)))
        gb_qv = over_dp(over_mp(jnp.stack(gb_qv)))
        gb_out = lax.psum(gb_out, ("dp", "mp"))
        gb_down = lax.psum(gb_down, ("dp", "mp"))
    grad_w_ada = lax.dot_general(
        act_all, dmod.reshape(dmod.shape[0], -1), (((0,), (0,)), ((), ())), precision=lax.Precision.HIGHEST
    ).reshape(width, 6, local_width)
    grad_b_ada = jnp.sum(dmod, axis=0)
    cond_term = lax.dot_general(
        own_dmod.reshape(items, -1),
        ada_flat.astype(f32),
        (((1,), (1,)), ((), ())),
        precision=lax.Precision.HIGHEST,
    )
    if paired:
        cond_term = cond_term + swap(cond_term, "mp", 1)
        cond_term = cond_term + swap(cond_term, "mp", 2)
    else:
        cond_term = lax.psum(cond_term, "mp")
    grad_condition = jax.vjp(jax.nn.silu, cond_value)[1](cond_term)[0]
    g_qkv = g_attn[: 3 * local_width].astype(f32).T.reshape(width, 3, local_width)
    return (
        output,
        grad_tokens,
        grad_condition,
        g_qkv,
        gb_qv.reshape(2, local_width),
        g_attn[3 * local_width :].astype(f32),
        gb_out,
        g_up.astype(f32),
        gb_up,
        g_down.astype(f32),
        gb_down,
        grad_w_ada,
        grad_b_ada,
    )


def solution(mesh):
    paired = dict(mesh.shape) == {"dp": 8, "mp": 4}
    return jax.shard_map(
        functools.partial(shards, paired),
        mesh=mesh,
        in_specs=(
            P(("dp", "mp"), None),
            P("dp", None),
            P("dp"),
            P("dp"),
            P("dp"),
            P("dp"),
            P("dp"),
            P(None, None, "mp"),
            P(None, "mp"),
            P("mp", None),
            P(),
            P(None, "mp"),
            P("mp"),
            P("mp", None),
            P(),
            P(None, None, "mp"),
            P(None, "mp"),
            P(("dp", "mp"), None),
        ),
        out_specs=(
            P(("dp", "mp"), None),
            P(("dp", "mp"), None),
            P("dp", None),
            P(None, None, "mp"),
            P(None, "mp"),
            P("mp", None),
            P(),
            P(None, "mp"),
            P("mp"),
            P("mp", None),
            P(),
            P(None, None, "mp"),
            P(None, "mp"),
        ),
        check_vma=False,
    )
```

time: 1450 us -> 863 us (0.60)
  waiting for transfers between devices: 792 us -> 64.1 us
  Pallas kernels: 0 us -> 236 us
  blocking collectives: 58.3 us -> 0 us
  matrix products: 329 us -> 303 us
  other arithmetic: 155 us -> 130 us
    psum x1 -> x0, waiting for transfers between devices: 307 us -> none  [shards(): lax.psum(grad_w_qkv.astype(jnp.bfloat16), 'dp').astype(jnp.float32)]
    all_gather x4 -> x0, waiting for transfers between devices: 236 us -> none  [the longest x1 64.3 us: shards(): full_one = lax.all_gather(grad_branch_one, 'mp', axis=0, tiled=True)]
    pallas_call x0 -> x1, Pallas kernels: none -> 236 us  [reduce_grads(): pl.pallas_call(functools.partial(reduce_kernel, count), out_shape=jax.Sha...]
    reduce_scatter x4 -> x0, waiting for transfers between devices: 236 us -> none  [the longest x1 77.9 us: shards(): lax.psum_scatter(jnp.dot(attended, w_out, preferred_element_type=jnp.floa...]
    dot_general x15 -> x43, matrix products: 212 us -> 145 us  [the longest x17 95.9 us: dot(): return jnp.dot(left, right, preferred_element_type=f32)]
    concatenate x0 -> x10, other arithmetic: none -> 62.5 us  [the longest x1 55.8 us: shards(): jnp.concatenate([jnp.stack(g_up), jnp.stack(g_down), jnp.stack(g_attn), t...]
    ppermute x0 -> x18, waiting for transfers between devices: none -> 45.8 us  [swap(): return lax.ppermute(values, axis, [(i, i ^ bit) for i in range(n)])]
    psum x2 -> x0, blocking collectives: 45.7 us -> none  [the longest x1 39.4 us: shards(): lax.psum(grad_qv_bias.astype(jnp.bfloat16), 'dp').astype(jnp.float32)]
  transfers between devices with their start and end apart: 10 -> 19, of which waited for: 10 -> 5; matrix products, arithmetic and copies ran while one was open for 10% -> 28% of each run, Pallas kernels for 0% -> 0%
where the time goes in v1:
time: 863 us; the launch traced here: 854 us
  matrix products  303 us (35%)
  Pallas kernels  236 us (27%)
  other arithmetic  130 us (15%)
  local copies, waits for them, and re-layouts  88.9 us (10%)
  waiting for transfers between devices  64.1 us (7%)
  between operations  18.3 us (2%)
  starting transfers between devices  13.5 us (2%)
    pallas_call x1, Pallas kernels, reduce_grads(): pl.pallas_call(functools.partial(reduce_kernel, count), out_shape=jax.Sha...  236 us
    dot_general x17, matrix products, dot(): return jnp.dot(left, right, preferred_element_type=f32)  95.9 us
    dot_general x16, matrix products, col_inner(): lax.dot_general(left, right, (((1,), (1,)), ((), ())), preferred_element_...  88.5 us
    dot_general x16, matrix products, row_inner(): lax.dot_general(left, right, (((0,), (0,)), ((), ())), preferred_element_...  69.4 us
    concatenate x1, other arithmetic, shards(): jnp.concatenate([jnp.stack(g_up), jnp.stack(g_down), jnp.stack(g_attn), t...  55.8 us
    ppermute x18, waiting for transfers between devices, swap(): return lax.ppermute(values, axis, [(i, i ^ bit) for i in range(n)])  45.8 us
    reshape x12, local copies, waits for them, and re-layouts, shards(): proj[:, j * local_width:(j + 1) * local_width]  24.6 us
    unnamed x2, waiting for transfers between devices  18.3 us
  transfers between devices with their start and end apart: 19, of which 5 were waited for; matrix products, arithmetic and copies ran while one was open for 28% of the time, Pallas kernels for 0%

profile of v1, /device:TPU:0, one launch (start us, length us, event | category | flops | bytes accessed | tf_op | source)
XLA Modules:
  0.0 853.5 jit_solution(8851672968370237495)
XLA Ops:
  33.3 18.3 %all-reduce.5.cloned.1.call-done = f32[21888]{0:T(1024)} async-done(((f32[21888]{0:T(1024)}), f32[21888]{0:T(1024)}) %all-reduce.5.cloned.1.call-update) | async-done | bytes 87568
  54.9 5.8 fusion.16
  74.2 5.0 convolution_add_fusion.2
  82.7 7.6 collective-permute-done.5
  93.3 17.2 %collective-permute-done.3 = bf16[576,864]{1,0:T(8,128)(2,1)S(1)} collective-permute-done((bf16[576,864]{1,0:T(8,128)(2,1)}, bf16[576,864]{1,0:T(8,128)(2,1)S(1)}, u32[]{:S(2)}, u32[]{:S(2)}) %collective-permute-start.3) | collective-permute-done | bytes 995360 | tf_op jit(solution)/shard_map/ppermute | solution.py:240
  125.6 4.7 add_convert_fusion.3
  151.6 4.5 copy.381
  158.0 6.4 convolution_add_fusion.1
  168.4 20.7 %collective-permute-done.13 = bf16[576,1152]{1,0:T(8,128)(2,1)S(1)} collective-permute-done((bf16[576,1152]{1,0:T(8,128)(2,1)}, bf16[576,1152]{1,0:T(8,128)(2,1)S(1)}, u32[]{:S(2)}, u32[]{:S(2)}) %collective-permute-start.13) | collective-permute-done | bytes 1327136 | tf_op jit(solution)/shard_map/ppermute | solution.py:240
  209.5 4.5 fusion.219
  214.9 5.5 add_convert_fusion
  227.6 7.5 fusion.235
  235.0 5.3 fusion.237
  240.3 8.0 fusion.197
  248.3 5.3 convolution_add_fusion.5
  253.6 4.8 fusion
  258.4 5.6 fusion.6
  264.0 7.1 fusion.233
  271.1 7.4 fusion.234
  278.6 4.8 fusion.1
  283.4 6.9 fusion.238
  290.4 7.9 fusion.198
  298.3 4.8 fusion.2
  305.5 5.7 fusion.5
  311.3 5.6 fusion.4
  316.9 5.8 convolution_add_fusion.3
  322.8 9.8 %fusion.232 = (bf16[1152]{0:T(1024)(128)(2,1)}, bf16[1024,1152]{1,0:T(8,128)(2,1)S(1)}) fusion(f32[1024,1152]{1,0:T(8,128)S(1)} %convolution_add_fusion.3, bf16[1152,1152]{1,0:T(8,128)(2,1)} %collective-permute-done.15, bf16[1024,1152]{1,0:T(8,128)(2,1)S(1)} %copy-done.36, f32[1152]{0:T(1024)S(1)} %copy-done.137, f32[1152]{0:T(1024)S(1)} %copy-done.134, ...), kind=kOutput, calls=%fused_computation.418 | convolution fusion | flops 2747399168 | bytes 12103936 | tf_op jit(solution)/shard_map/dot_general | solution.py:54
  332.7 7.8 fusion.239
  340.5 10.0 %select_reduce_fusion.2 = (bf16[1152]{0:T(1024)(128)(2,1)}, f32[1024]{0:T(1024)S(1)}, bf16[1152]{0:T(1024)(128)(2,1)}, f32[1024]{0:T(1024)S(1)}, bf16[1152]{0:T(...) fusion(pred[1024]{0:T(1024)(128)(4,1)S(1)} %copy-done.125, f32[1024]{0:T(1024)S(1)} %copy-done.120, ...), kind=kOutput, calls=%fused_computation.90 | convolution fusion | flops 2746804224 | bytes 28643328 | tf_op jit(solution)/shard_map/dot_general | solution.py:54
  350.6 5.2 convert_reduce_fusion.2
  362.4 3.9 fusion.133
  376.0 3.9 fusion.130
  390.8 3.9 fusion.127
  405.8 3.9 fusion.124
  417.0 3.9 convolution_convert_fusion.11
  421.0 4.5 fusion.240
  446.2 4.2 convolution_convert_fusion.8
  452.8 7.3 fusion.3
  460.0 8.0 fusion.7
  468.0 4.6 fusion.241
  475.9 4.8 add_add_fusion
  480.8 7.7 fusion.199
  488.7 19.9 %select_reduce_fusion.8 = (bf16[1152]{0:T(1024)(128)(2,1)S(1)}, f32[1024]{0:T(1024)}, bf16[1152]{0:T(1024)(128)(2,1)S(1)}, f32[1024]{0:T(1024)}, bf16[1152]{0:T(...) fusion(f32[1024,1152]{1,0:T(8,128)} %add_add_fusion, ...), kind=kOutput, calls=%fused_computation.96 | convolution fusion | flops 2782187520 | bytes 47543040 | tf_op jit(solution)/shard_map/dot_general | solution.py:46
  527.1 55.8 %pad_maximum_fusion.g_ref = bf16[4,3584,1152]{2,1,0:T(8,128)(2,1)} fusion(bf16[4,128,1152]{2,1,0:T(8,128)(2,1)S(1)} %fusion.138, bf16[1,1152,1152]{2,1,0:T(8,128)(2,1)} %maximum_bitcast_fusion.3, bf16[1,1152,1152]{2,1,0:T(8,128)(2,1)} %maximum_bitcast_fusion.2, bf16[1,1152,1152]{2,1,0:T(8,128)(2,1)} %maximum_bitcast_fusion.1, ...), kind=kLoop, calls=%fused_computation.2 | loop fusion | flops 429391872 | bytes 66060288 | tf_op jit(solution)/shard_map/concatenate | solution.py:438
  582.9 236.2 %shard_map.273 = bf16[3584,1152]{1,0:T(8,128)(2,1)S(1)} custom-call(bf16[4,3584,1152]{2,1,0:T(8,128)(2,1)} %pad_maximum_fusion.g_ref), custom_call_target="tpu_custom_call" | custom-call | tf_op jit(solution)/shard_map/pallas_call | solution.py:209
  819.1 5.2 slice_convert_fusion
  828.6 5.4 fusion.175
  834.8 5.9 fusion.21
  (647 shorter events, 220.5 us)
Async XLA Ops:
  7.2 44.4 %all-reduce.5.cloned.1.call-start = ((), (), s32[]{:S(2)}) async-start(), calls=%async_computation | async-start | bytes 180224
  7.3 116.9 %collective-permute-start = (bf16[1152,864]{0,1:T(8,128)(2,1)}, bf16[1152,864]{0,1:T(8,128)(2,1)}, u32[]{:S(2)}, u32[]{:S(2)}) collective-permute-start(bf16[1152,864]{0,1:T(8,128)(2,1)} %bitcast.330), channel_id=1, source_target_pairs={{0,1},{1,0},{2,3},{3,2},{4,5},{5,4},{6,7},{7,6},{8,9},{9,8},{10,11... | collective-permute-start | bytes 5971976 | tf_op jit(solution)/shard_map/ppermute | solution.py:240
  11.3 14.2 %copy-start.166 = (s32[16]{0:T(128)S(1)}, s32[16]{0:T(128)}, u32[]{:S(2)}) copy-start(s32[16]{0:T(128)} %param.23) | copy-start | bytes 196
  11.3 14.9 %copy-start.10 = (bf16[1024,1152]{1,0:T(8,128)(2,1)S(1)}, bf16[1024,1152]{1,0:T(8,128)(2,1)}, u32[]{:S(2)}) copy-start(bf16[1024,1152]{1,0:T(8,128)(2,1)} %param.18) | copy-start | bytes 7077892
  11.3 69.5 %collective-permute-start.2 = (bf16[576,864]{1,0:T(8,128)(2,1)}, bf16[576,864]{1,0:T(8,128)(2,1)}, u32[]{:S(2)}, u32[]{:S(2)}) collective-permute-start(bf16[576,864]{1,0:T(8,128)(2,1)} %copy.375), channel_id=1, source_target_pairs={{0,2},{1,3},{2,0},{3,1},{4,6},{5,7},{6,4},{7,5},{8,10},{9,11},{10,... | collective-permute-start | bytes 2985992 | tf_op jit(solution)/shard_map/ppermute | solution.py:240
  19.9 137.4 %collective-permute-start.1 = (bf16[288,1152]{1,0:T(8,128)(2,1)}, bf16[288,1152]{1,0:T(8,128)(2,1)}, u32[]{:S(2)}, u32[]{:S(2)}) collective-permute-start(bf16[288,1152]{1,0:T(8,128)(2,1)} %param.27), channel_id=1, source_target_pairs={{0,1},{1,0},{2,3},{3,2},{4,5},{5,4},{6,7},{7,6},{8,9},{9,8},{10,11... | collective-permute-start | bytes 1990664 | tf_op jit(solution)/shard_map/ppermute | solution.py:240
  21.9 57.4 %collective-permute-start.4 = (bf16[144,1152]{1,0:T(8,128)(2,1)}, bf16[144,1152]{1,0:T(8,128)(2,1)}, u32[]{:S(2)}, u32[]{:S(2)}) collective-permute-start(bf16[144,1152]{1,0:T(8,128)(2,1)} %constant_dynamic-slice_fusion.2), channel_id=1, source_target_pairs={{0,2},{1,3},{2,0},{3,1},{4,6},{5,7},{6,4},{7,5},{8,10},{9,11},{10,... | collective-permute-start | bytes 995336 | tf_op jit(solution)/shard_map/ppermute | solution.py:240
  22.2 226.1 %collective-permute-start.8 = (bf16[1152,1152]{1,0:T(8,128)(2,1)}, bf16[1152,1152]{1,0:T(8,128)(2,1)}, u32[]{:S(2)}, u32[]{:S(2)}) collective-permute-start(bf16[1152,1152]{1,0:T(8,128)(2,1)} %param.29), channel_id=1, source_target_pairs={{0,1},{1,0},{2,3},{3,2},{4,5},{5,4},{6,7},{7,6},{8,9},{9,8},{10,11... | collective-permute-start | bytes 7962632 | tf_op jit(solution)/shard_map/ppermute | solution.py:240
  26.2 28.7 %copy-start.124 = (pred[1024]{0:T(1024)(128)(4,1)}, pred[1024]{0:T(1024)(128)(4,1)S(1)}, u32[]{:S(2)}) copy-start(pred[1024]{0:T(1024)(128)(4,1)S(1)} %get-tuple-element.93) | copy-start | bytes 3076
  26.6 34.1 %copy-start.114 = (f32[1024]{0:T(1024)}, f32[1024]{0:T(1024)S(1)}, u32[]{:S(2)}) copy-start(f32[1024]{0:T(1024)S(1)} %broadcast_multiply_fusion.5) | copy-start | bytes 12292
  27.3 33.4 %copy-start.121 = (f32[1024]{0:T(1024)}, f32[1024]{0:T(1024)S(1)}, u32[]{:S(2)}) copy-start(f32[1024]{0:T(1024)S(1)} %add_rsqrt_fusion.1) | copy-start | bytes 12292
  32.1 28.6 %copy-start.146 = (s32[1024]{0:T(1024)}, s32[1024]{0:T(1024)S(1)}, u32[]{:S(2)}) copy-start(s32[1024]{0:T(1024)S(1)} %pad_clamp_fusion) | copy-start | bytes 12292
  53.6 155.8 %copy-start.104 = (f32[1152]{0:T(1024)}, f32[1152]{0:T(1024)S(1)}, u32[]{:S(2)}) copy-start(f32[1152]{0:T(1024)S(1)} %get-tuple-element.43) | copy-start | bytes 13828
  53.6 155.8 %copy-start.106 = (f32[1152]{0:T(1024)}, f32[1152]{0:T(1024)S(1)}, u32[]{:S(2)}) copy-start(f32[1152]{0:T(1024)S(1)} %get-tuple-element.44) | copy-start | bytes 13828
  79.2 32.8 %copy-start.71 = (bf16[1024,1152]{1,0:T(8,128)(2,1)S(1)}, bf16[1024,1152]{1,0:T(8,128)(2,1)}, u32[]{:S(2)}) copy-start(bf16[1024,1152]{1,0:T(8,128)(2,1)} %copy-done.70) | copy-start | bytes 7077892
  79.2 32.8 %copy-start.154 = (f32[864]{0:T(1024)S(1)}, f32[864]{0:T(1024)}, u32[]{:S(2)}) copy-start(f32[864]{0:T(1024)} %get-tuple-element.49) | copy-start | bytes 10372
  79.2 11.0 %collective-permute-start.5 = (bf16[144,1152]{1,0:T(8,128)(2,1)}, bf16[144,1152]{1,0:T(8,128)(2,1)S(1)}, u32[]{:S(2)}, u32[]{:S(2)}) collective-permute-start(bf16[144,1152]{1,0:T(8,128)(2,1)} %collective-permute-done.4), channel_id=1, source_target_pairs={{0,4},{4,0},{8,12},{12,8},{16,20},{20,16},{24,28},{28,24},{1,5},{5... | collective-permute-start | bytes 995336 | tf_op jit(solution)/shard_map/ppermute | solution.py:240
  80.8 29.8 %collective-permute-start.3 = (bf16[576,864]{1,0:T(8,128)(2,1)}, bf16[576,864]{1,0:T(8,128)(2,1)S(1)}, u32[]{:S(2)}, u32[]{:S(2)}) collective-permute-start(bf16[576,864]{1,0:T(8,128)(2,1)} %collective-permute-done.2), channel_id=1, source_target_pairs={{0,4},{4,0},{8,12},{12,8},{16,20},{20,16},{24,28},{28,24},{1,5},{5... | collective-permute-start | bytes 2985992 | tf_op jit(solution)/shard_map/ppermute | solution.py:240
  90.3 32.9 %collective-permute-start.10 = (bf16[576,1152]{1,0:T(8,128)(2,1)}, bf16[576,1152]{1,0:T(8,128)(2,1)}, u32[]{:S(2)}, u32[]{:S(2)}) collective-permute-start(bf16[576,1152]{1,0:T(8,128)(2,1)} %constant_dynamic-slice_fusion.1), channel_id=1, source_target_pairs={{0,2},{1,3},{2,0},{3,1},{4,6},{5,7},{6,4},{7,5},{8,10},{9,11},{10,... | collective-permute-start | bytes 3981320 | tf_op jit(solution)/shard_map/ppermute | solution.py:240
  92.3 18.2 %copy-start.30 = (bf16[144,1152]{1,0:T(8,128)(2,1)}, bf16[144,1152]{1,0:T(8,128)(2,1)S(1)}, u32[]{:S(2)}) copy-start(bf16[144,1152]{1,0:T(8,128)(2,1)S(1)} %get-tuple-element.90) | copy-start | bytes 995332
  92.3 18.2 %copy-start.33 = (bf16[144,1152]{1,0:T(8,128)(2,1)}, bf16[144,1152]{1,0:T(8,128)(2,1)S(1)}, u32[]{:S(2)}) copy-start(bf16[144,1152]{1,0:T(8,128)(2,1)S(1)} %get-tuple-element.91) | copy-start | bytes 995332
  110.5 160.6 %collective-permute-start.9 = (bf16[1152,1152]{1,0:T(8,128)(2,1)}, bf16[1152,1152]{1,0:T(8,128)(2,1)}, u32[]{:S(2)}, u32[]{:S(2)}) collective-permute-start(bf16[1152,1152]{1,0:T(8,128)(2,1)} %param.31), channel_id=1, source_target_pairs={{0,1},{1,0},{2,3},{3,2},{4,5},{5,4},{6,7},{7,6},{8,9},{9,8},{10,11... | collective-permute-start | bytes 7962632 | tf_op jit(solution)/shard_map/ppermute | solution.py:240
  112.0 38.1 %copy-start.13 = (bf16[576,864]{1,0:T(8,128)(2,1)}, bf16[576,864]{1,0:T(8,128)(2,1)S(1)}, u32[]{:S(2)}) copy-start(bf16[576,864]{1,0:T(8,128)(2,1)S(1)} %get-tuple-element.76) | copy-start | bytes 2985988
  123.2 34.1 %collective-permute-start.12 = (bf16[576,1152]{1,0:T(8,128)(2,1)}, bf16[576,1152]{1,0:T(8,128)(2,1)}, u32[]{:S(2)}, u32[]{:S(2)}) collective-permute-start(bf16[576,1152]{1,0:T(8,128)(2,1)} %constant_dynamic-slice_fusion), channel_id=1, source_target_pairs={{0,2},{1,3},{2,0},{3,1},{4,6},{5,7},{6,4},{7,5},{8,10},{9,11},{10,... | collective-permute-start | bytes 3981320 | tf_op jit(solution)/shard_map/ppermute | solution.py:240
  124.2 40.2 %collective-permute-start.11 = (bf16[576,1152]{1,0:T(8,128)(2,1)}, bf16[576,1152]{1,0:T(8,128)(2,1)}, u32[]{:S(2)}, u32[]{:S(2)}) collective-permute-start(bf16[576,1152]{1,0:T(8,128)(2,1)} %collective-permute-done.10), channel_id=1, source_target_pairs={{0,4},{4,0},{8,12},{12,8},{16,20},{20,16},{24,28},{28,24},{1,5},{5... | collective-permute-start | bytes 3981320 | tf_op jit(solution)/shard_map/ppermute | solution.py:240
  157.3 49.1 %collective-permute-start.7 = (bf16[288,1152]{1,0:T(8,128)(2,1)}, bf16[288,1152]{1,0:T(8,128)(2,1)}, u32[]{:S(2)}, u32[]{:S(2)}) collective-permute-start(bf16[288,1152]{1,0:T(8,128)(2,1)} %pad_maximum_fusion.4), channel_id=1, source_target_pairs={{0,1},{1,0},{2,3},{3,2},{4,5},{5,4},{6,7},{7,6},{8,9},{9,8},{10,11... | collective-permute-start | bytes 1990664 | tf_op jit(solution)/shard_map/ppermute | solution.py:240
  157.3 31.7 %collective-permute-start.13 = (bf16[576,1152]{1,0:T(8,128)(2,1)}, bf16[576,1152]{1,0:T(8,128)(2,1)S(1)}, u32[]{:S(2)}, u32[]{:S(2)}) collective-permute-start(bf16[576,1152]{1,0:T(8,128)(2,1)} %collective-permute-done.12), channel_id=1, source_target_pairs={{0,4},{4,0},{8,12},{12,8},{16,20},{20,16},{24,28},{28,24},{1,5},{5... | collective-permute-start | bytes 3981320 | tf_op jit(solution)/shard_map/ppermute | solution.py:240
  164.4 28.2 %collective-permute-start.6 = (bf16[1152,864]{0,1:T(8,128)(2,1)S(1)}, bf16[1152,864]{0,1:T(8,128)(2,1)S(1)}, u32[]{:S(2)}, u32[]{:S(2)}) collective-permute-start(bf16[1152,864]{0,1:T(8,128)(2,1)S(1)} %copy-done.78), channel_id=1, source_target_pairs={{0,1},{1,0},{2,3},{3,2},{4,5},{5,4},{6,7},{7,6},{8,9},{9,8},{10,11... | collective-permute-start | bytes 5971976 | tf_op jit(solution)/shard_map/ppermute | solution.py:240
  166.5 22.6 %copy-start.22 = (bf16[576,1152]{1,0:T(8,128)(2,1)}, bf16[576,1152]{1,0:T(8,128)(2,1)S(1)}, u32[]{:S(2)}) copy-start(bf16[576,1152]{1,0:T(8,128)(2,1)S(1)} %get-tuple-element.72) | copy-start | bytes 3981316
  166.5 22.6 %copy-start.24 = (bf16[576,1152]{1,0:T(8,128)(2,1)}, bf16[576,1152]{1,0:T(8,128)(2,1)S(1)}, u32[]{:S(2)}) copy-start(bf16[576,1152]{1,0:T(8,128)(2,1)S(1)} %get-tuple-element.73) | copy-start | bytes 3981316
  168.4 24.8 %copy-start.72 = (bf16[1024,1152]{1,0:T(8,128)(2,1)S(1)}, bf16[1024,1152]{1,0:T(8,128)(2,1)}, u32[]{:S(2)}) copy-start(bf16[1024,1152]{1,0:T(8,128)(2,1)} %copy-done.70) | copy-start | bytes 7077892
  168.4 24.8 %copy-start.152 = (f32[864]{0:T(1024)S(1)}, f32[864]{0:T(1024)}, u32[]{:S(2)}) copy-start(f32[864]{0:T(1024)} %get-tuple-element.50) | copy-start | bytes 10372
  189.1 127.8 %collective-permute-start.14 = (bf16[1152,1152]{1,0:T(8,128)(2,1)}, bf16[1152,1152]{1,0:T(8,128)(2,1)}, u32[]{:S(2)}, u32[]{:S(2)}) collective-permute-start(bf16[1152,1152]{1,0:T(8,128)(2,1)} %pad_maximum_fusion.1), channel_id=1, source_target_pairs={{0,1},{1,0},{2,3},{3,2},{4,5},{5,4},{6,7},{7,6},{8,9},{9,8},{10,11... | collective-permute-start | bytes 7962632 | tf_op jit(solution)/shard_map/ppermute | solution.py:240
  192.6 130.2 %collective-permute-start.15 = (bf16[1152,1152]{1,0:T(8,128)(2,1)}, bf16[1152,1152]{1,0:T(8,128)(2,1)}, u32[]{:S(2)}, u32[]{:S(2)}) collective-permute-start(bf16[1152,1152]{1,0:T(8,128)(2,1)} %pad_maximum_fusion.2), channel_id=1, source_target_pairs={{0,1},{1,0},{2,3},{3,2},{4,5},{5,4},{6,7},{7,6},{8,9},{9,8},{10,11... | collective-permute-start | bytes 7962632 | tf_op jit(solution)/shard_map/ppermute | solution.py:240
  220.4 96.5 %copy-start.50 = (bf16[1024,1152]{1,0:T(8,128)(2,1)}, bf16[1024,1152]{1,0:T(8,128)(2,1)S(1)}, u32[]{:S(2)}) copy-start(bf16[1024,1152]{1,0:T(8,128)(2,1)S(1)} %add_convert_fusion) | copy-start | bytes 7077892
  224.0 40.1 %copy-start.170 = (f32[1024,1152]{1,0:T(8,128)}, f32[1024,1152]{1,0:T(8,128)S(1)}, u32[]{:S(2)}) copy-start(f32[1024,1152]{1,0:T(8,128)S(1)} %convolution_add_fusion.4) | copy-start | bytes 14155780
  316.9 23.5 %slice-start = ((s8[4718592]{0:T(1024)(128)(4,1)}), s8[4194304]{0:T(1024)(128)(4,1)S(1)}, s32[]{:S(2)}) async-start(s8[4718592]{0:T(1024)(128)(4,1)} %bitcast.288), calls=%async_computation.1 | async-start | bytes 8388608
  322.8 17.7 %slice-start.1 = ((s8[4718592]{0:T(1024)(128)(4,1)}), s8[524288]{0:T(1024)(128)(4,1)S(1)}, s32[]{:S(2)}) async-start(s8[4718592]{0:T(1024)(128)(4,1)} %bitcast.288), calls=%async_computation.2 | async-start | bytes 1048576
  488.6 20.5 %copy-start.158 = (bf16[1152]{0:T(1024)(128)(2,1)S(1)}, bf16[1152]{0:T(1024)(128)(2,1)}, u32[]{:S(2)}) copy-start(bf16[1152]{0:T(1024)(128)(2,1)} %get-tuple-element.25) | copy-start | bytes 6916
  488.6 20.6 %copy-start.157 = (bf16[1152]{0:T(1024)(128)(2,1)S(1)}, bf16[1152]{0:T(1024)(128)(2,1)}, u32[]{:S(2)}) copy-start(bf16[1152]{0:T(1024)(128)(2,1)} %get-tuple-element.26) | copy-start | bytes 6916
  488.6 20.7 %copy-start.156 = (bf16[1152]{0:T(1024)(128)(2,1)S(1)}, bf16[1152]{0:T(1024)(128)(2,1)}, u32[]{:S(2)}) copy-start(bf16[1152]{0:T(1024)(128)(2,1)} %get-tuple-element.15) | copy-start | bytes 6916
  488.6 20.8 %copy-start.155 = (bf16[1152]{0:T(1024)(128)(2,1)S(1)}, bf16[1152]{0:T(1024)(128)(2,1)}, u32[]{:S(2)}) copy-start(bf16[1152]{0:T(1024)(128)(2,1)} %get-tuple-element.13) | copy-start | bytes 6916
  488.6 25.2 %copy-start.131 = (bf16[1,1152]{1,0:T(2,128)(2,1)S(1)}, bf16[1,1152]{1,0:T(2,128)(2,1)}, u32[]{:S(2)}) copy-start(bf16[1,1152]{1,0:T(2,128)(2,1)} %stack.184) | copy-start | bytes 6916
  488.7 25.2 %copy-start.132 = (bf16[1,1152]{1,0:T(2,128)(2,1)S(1)}, bf16[1,1152]{1,0:T(2,128)(2,1)}, u32[]{:S(2)}) copy-start(bf16[1,1152]{1,0:T(2,128)(2,1)} %stack.183) | copy-start | bytes 6916
  488.7 25.2 %copy-start.133 = (bf16[1,1152]{1,0:T(2,128)(2,1)S(1)}, bf16[1,1152]{1,0:T(2,128)(2,1)}, u32[]{:S(2)}) copy-start(bf16[1,1152]{1,0:T(2,128)(2,1)} %stack.182) | copy-start | bytes 6916
  488.7 28.9 %copy-start.84 = (bf16[288,1152]{1,0:T(8,128)(2,1)S(1)}, bf16[288,1152]{1,0:T(8,128)(2,1)}, u32[]{:S(2)}) copy-start(bf16[288,1152]{1,0:T(8,128)(2,1)} %convolution_convert_fusion.15) | copy-start | bytes 1990660
  834.7 6.6 collective-permute-start.16
  841.3 4.5 collective-permute-start.17
  (153 other events, 786.3 us)
Sparse Core Ops, SparseCore 0:
  20.0 31.5 all-reduce.4

commit v2 on v1

v2 whole, which is shorter than its diff:
```python
import functools

import jax
import jax.numpy as jnp
from jax import lax
from jax.experimental import pallas as pl
from jax.experimental.pallas import tpu as pltpu
from jax.sharding import PartitionSpec as P

HEAD = 72
SLOT = 256
CHUNK = 128
UNITS = 4
OUT_SLOTS = 6
MESH = pl.DeviceIdType.MESH
epsilon = 1e-06
f32 = jnp.float32
bf16 = jnp.bfloat16


def frame_tables(grid_rows, grid_cols, frame_start, frame_item, used, first, length):
    rows = first + jnp.arange(length, dtype=jnp.int32)[:, None]
    slots = jnp.arange(grid_rows.shape[0], dtype=jnp.int32)[None, :]
    ends = (frame_start + grid_rows * grid_cols)[None, :]
    inside = (rows >= frame_start[None, :]) & (rows < ends) & (slots < used)
    frame_id = jnp.sum(jnp.where(inside, slots + 1, 0), axis=1) - 1
    item_id = jnp.sum(jnp.where(inside, frame_item[None, :], 0), axis=1)
    return (frame_id, item_id)


def normal(values):
    centred = values - jnp.mean(values, axis=-1, keepdims=True)
    rstd = lax.rsqrt(jnp.mean(centred * centred, axis=-1, keepdims=True) + epsilon)
    return centred * rstd, rstd


def normal_back(grad, scale, normed, rstd):
    u = grad * (1.0 + scale)
    return rstd * (
        u
        - jnp.mean(u, axis=-1, keepdims=True)
        - normed * jnp.mean(u * normed, axis=-1, keepdims=True)
    )


def dot(left, right):
    return jnp.dot(left, right, preferred_element_type=f32)


def pieces_of(ff):
    if ff % 128 or ff <= 640:
        return [(0, ff)]
    return [(0, 640), (640, ff - 640)]


def rows_at(i, size):
    return pl.ds(pl.multiple_of(i * size, size), size)


def pick(item_col, mod_ref, k):
    total = mod_ref[0, k : k + 1, :]
    for item in range(1, mod_ref.shape[0]):
        total = jnp.where(item_col == item, mod_ref[item, k : k + 1, :], total)
    return total


def add_by_item(sums_ref, k, item_col, values):
    for item in range(sums_ref.shape[0]):
        part = jnp.sum(jnp.where(item_col == item, values, 0.0), axis=0, keepdims=True)
        sums_ref[item, k : k + 1, :] += part


def tn(left, right):
    return lax.dot_general(left, right, (((0,), (0,)), ((), ())), preferred_element_type=f32)


def nt(left, right):
    return lax.dot_general(left, right, (((1,), (1,)), ((), ())), preferred_element_type=f32)


class Shard:
    def __init__(self, own, others, a, m, part, target, sem):
        self.own, self.others, self.a, self.m, self.part = own, others, a, m, part
        self.target, self.sem = target, sem

    def copy(self, source):
        return pltpu.make_async_copy(source.at[self.part], self.target, self.sem)

    def start(self):
        if self.own is None:
            self.copy(self.others.at[self.a, self.m]).start()
            return

        @pl.when(self.m == 0)
        def _():
            self.copy(self.own[self.a]).start()

        @pl.when(self.m > 0)
        def _():
            self.copy(self.others.at[self.a, self.m - 1]).start()

    def wait(self):
        source = self.others.at[self.a, 0] if self.own is None else self.own[self.a]
        self.copy(source).wait()


def pair_bias(id_col, id_row):
    shape = (SLOT, SLOT)
    one = lax.broadcasted_iota(jnp.int32, shape, 0) == lax.broadcasted_iota(jnp.int32, shape, 1)
    same = (id_col == id_row) & (id_col >= 0)
    return jnp.where(same | one, 0.0, -1e30)


def gather_ticks(own, w_all, sends, recvs):
    dp, mp = lax.axis_index("dp"), lax.axis_index("mp")
    core, yb = mp % 2, dp % 2
    xb, z0 = mp // 2, (dp // 2) % 2
    sib = (dp, mp + 1 - 2 * core)
    xn = (dp, mp + 2 - 4 * xb)
    yn = (dp + 1 - 2 * yb, mp)
    zn = (dp + 2 - 4 * z0, mp)
    rows = w_all.shape[2]
    part = rows // (UNITS * 9)
    count = len(own) * UNITS

    def greet():
        barrier = pltpu.get_barrier_semaphore()
        for peer in (sib, xn, yn, zn):
            pl.semaphore_signal(barrier, inc=1, device_id=peer, device_id_type=MESH)
        pl.semaphore_wait(barrier, 4)

    def remote(stage, slot, src, dst, peer):
        return pltpu.make_async_remote_copy(
            src_ref=src,
            dst_ref=dst,
            send_sem=sends.at[stage, slot],
            recv_sem=recvs.at[stage, slot],
            device_id=peer,
            device_id_type=MESH,
        )

    def near(a):
        return remote(7, a, own[a], w_all.at[a, 0], sib)

    def span(c, at, size):
        return pl.ds(pl.multiple_of((c % UNITS) * 9 * part + at * part, part), size * part)

    by_z, by_y = z0 * 2 + yb, 4 + yb * 2 + z0
    pair_z, pair_y = z0 * 2, 4 + yb * 2

    def x_copies(a, c):
        places = (span(c, by_z, 1), span(c, by_y, 1), span(c, 8, 1))
        return [
            remote(k, c % 2, own[a].at[place], w_all.at[a, 1, place], xn)
            for k, place in enumerate(places)
        ]

    def hand(stage, c, at, size, peer, to=1):
        src = w_all.at[c // UNITS, 1, span(c, at, size)]
        return remote(stage, c % 2, src, w_all.at[c // UNITS, to, span(c, at, size)], peer)

    def second(c):
        return [hand(3, c, by_z, 1, yn), hand(4, c, by_y, 1, zn)]

    def third(c):
        return [hand(5, c, pair_z, 2, zn), hand(6, c, pair_y, 2, yn)]

    def across(c):
        return hand(8, c, 0, 9, sib, 2)

    def begin():
        greet()
        for a in range(len(own)):
            near(a).start()

    def ready(a):
        near(a).wait()

    def tick(i):
        def stage(lag, work):
            c = i - lag

            @pl.when((c >= 0) & (c < count))
            def _():
                work(c)

        def leave(c):
            across(c).wait()

        def go_across(c):
            for copy in third(c):
                copy.wait()
            across(c).start()

        def go_third(c):
            for copy in second(c):
                copy.wait()
            for copy in third(c):
                copy.start()

        def go_second(c):
            for a in range(len(own)):

                @pl.when(c // UNITS == a)
                def _(a=a):
                    for copy in x_copies(a, c):
                        copy.wait()

            for copy in second(c):
                copy.start()

        def go_first(c):
            for a in range(len(own)):

                @pl.when(c // UNITS == a)
                def _(a=a):
                    for copy in x_copies(a, c):
                        copy.start()

        stage(4, leave)
        stage(3, go_across)
        stage(2, go_third)
        stage(1, go_second)
        stage(0, go_first)

    return begin, ready, tick, count + 5


def attend_kernel(n, heads, paired, *refs):
    if paired:
        tokens, item, ids, ids_row, mod, bias, b_out, *refs = refs
        *own, normed_ref, branch_ref, qkv_hbm, lse_ref, att_hbm, w_all, w_buf, qkv_buf, att_buf, w_sem, qkv_sem, att_sem = refs[:-2]
        begin, ready, tick, ticks = gather_ticks(own, w_all, *refs[-2:])
        begin()
    else:
        (
            tokens, item, ids, ids_row, mod, bias, b_out, w_all, normed_ref, branch_ref, qkv_hbm, lse_ref, att_hbm,
            w_buf, qkv_buf, att_buf, w_sem, qkv_sem, att_sem,
        ) = refs
        own = None
    rows, width = tokens.shape
    frames = rows // SLOT
    lw = heads * HEAD
    scale = HEAD ** (-0.5)

    def w_copy(m):
        return Shard(own, w_all, 0, m, slice(None), w_buf.at[m % 2], w_sem.at[m % 2])

    def qkv_copy(m):
        return pltpu.make_async_copy(qkv_buf.at[m % 2], qkv_hbm.at[m], qkv_sem.at[m % 2])

    def att_copy(m):
        return pltpu.make_async_copy(att_buf.at[m % 2], att_hbm.at[m], att_sem.at[m % 2])

    w_copy(0).start()

    def first(f, carry):
        if paired:
            tick(f)
        at = rows_at(f, SLOT)
        col = item[at, :]
        normed, _ = normal(tokens[at, :].astype(f32))
        normed_ref[at, :] = (normed * (1.0 + pick(col, mod, 1)) + pick(col, mod, 0)).astype(bf16)
        branch_ref[at, :] = jnp.broadcast_to(b_out[...], (SLOT, width))
        return carry

    lax.fori_loop(0, frames, first, 0)
    if paired:
        ready(0)

    def shard(m, carry):
        slot = m % 2
        w_copy(m).wait()

        @pl.when(m + 1 < (2 if paired else n))
        def _():
            w_copy(m + 1).start()

        @pl.when(m >= 2)
        def _():
            qkv_copy(m - 2).wait()
            att_copy(m - 2).wait()

        def frame(f, c):
            if paired:
                tick(frames + m * frames + f)
            at = rows_at(f, SLOT)
            proj = nt(w_buf[slot, : 3 * lw, :], normed_ref[at, :]) + bias[m]
            pairs = pair_bias(ids[at, :], ids_row[pl.ds(f, 1), :])
            outs = []
            for h in range(heads):
                q, k, v = (
                    proj[j * lw + h * HEAD : j * lw + (h + 1) * HEAD].astype(bf16)
                    for j in range(3)
                )
                qkv_buf[slot, h, :, at] = q
                qkv_buf[slot, heads + h, :, at] = k
                qkv_buf[slot, 2 * heads + h, :, at] = v
                scores = tn(k, q) * scale + pairs
                peak = jnp.max(scores, axis=0, keepdims=True)
                weights = jnp.exp(scores - peak)
                total = jnp.sum(weights, axis=0, keepdims=True)
                lse_ref[m, h : h + 1, at] = peak + jnp.log(total)
                probs = (weights * (1.0 / total)).astype(bf16)
                outs.append(jnp.dot(v, probs, preferred_element_type=f32))
            att = jnp.concatenate(outs, axis=0).astype(bf16)
            att_buf[slot, :, at] = att
            branch_ref[at, :] += tn(att, w_buf[slot, 3 * lw :, :])
            return c

        lax.fori_loop(0, frames, frame, 0)
        qkv_copy(m).start()
        att_copy(m).start()
        if paired:
            @pl.when((m >= 1) & (m + 1 < n))
            def _():
                w_copy(m + 1).start()

        return carry

    lax.fori_loop(0, n, shard, 0)
    if paired:

        def drain(i, carry):
            tick(i)
            return carry

        lax.fori_loop(frames * (n + 1), ticks, drain, 0)
        ready(1)
        ready(2)
    for m in range(max(n - 2, 0), n):
        qkv_copy(m).wait()
        att_copy(m).wait()


def attend(tokens, item, ids, mod, bias, b_out, weights, paired):
    rows, width = tokens.shape
    n = bias.shape[0]
    depth = weights[0].shape[-2]
    lw = depth // 4
    heads = lw // HEAD
    vmem = pl.BlockSpec(memory_space=pltpu.VMEM)
    hbm = pl.BlockSpec(memory_space=pl.ANY)
    return pl.pallas_call(
        functools.partial(attend_kernel, n, heads, paired),
        out_shape=(
            jax.ShapeDtypeStruct((rows, width), bf16),
            jax.ShapeDtypeStruct((rows, width), f32),
            jax.ShapeDtypeStruct((n, 3 * heads, HEAD, rows), bf16),
            jax.ShapeDtypeStruct((n, heads, rows), f32),
            jax.ShapeDtypeStruct((n, lw, rows), bf16),
        )
        + paired * (jax.ShapeDtypeStruct((3, n - 1, depth, width), bf16),),
        in_specs=[vmem] * 7 + [hbm] * len(weights),
        out_specs=(vmem, vmem, hbm, vmem, hbm) + paired * (hbm,),
        scratch_shapes=[
            pltpu.VMEM((2, depth, width), bf16),
            pltpu.VMEM((2, 3 * heads, HEAD, rows), bf16),
            pltpu.VMEM((2, lw, rows), bf16),
            pltpu.SemaphoreType.DMA((2,)),
            pltpu.SemaphoreType.DMA((2,)),
            pltpu.SemaphoreType.DMA((2,)),
        ]
        + paired
        * [
            pltpu.SemaphoreType.DMA((9, 3)),
            pltpu.SemaphoreType.DMA((9, 3)),
        ],
        compiler_params=pltpu.CompilerParams(
            collective_id=1 if paired else None, has_side_effects=paired, vmem_limit_bytes=56 << 20
        ),
    )(tokens, item[:, None], ids[:, None], ids.reshape(-1, SLOT), mod, bias, b_out, *weights)


def gelu_both(v):
    c = (2.0 / jnp.pi) ** 0.5
    square = v * v
    t = jnp.tanh(c * v * (1.0 + 0.044715 * square))
    half = 0.5 * (1.0 + t)
    slope = half + 0.5 * v * (1.0 - t * t) * (c * (1.0 + 3.0 * 0.044715 * square))
    return v * half, slope


def back_kernel(
    n, heads, pieces, tile, paired,
    tokens, upstream, branch_one, normed_hbm, item, ids, ids_row, mod, b_up, b_down, lse,
    w_all, own_attn, own_up, own_down, qkv_hbm, att_hbm,
    output_ref, gtok_ref, sums_ref, gb_down, gb_out, gb_up, gb_qv, g_all,
    n_buf, d_buf, acc_a, acc_b, up_buf, down_buf, w_buf, hid_buf, dpre_buf, stage_buf, qkv_buf, att_buf, dproj_buf,
    up_sem, down_sem, n_sem, stage_sem, w_sem, qkv_sem, att_sem,
):
    rows, width = tokens.shape
    lw = heads * HEAD
    frames = rows // SLOT
    scale = HEAD ** (-0.5)
    tiles = rows // tile
    own = (own_attn, own_up, own_down) if paired else None
    ff = w_all.shape[2]
    sums_ref[...] = jnp.zeros_like(sums_ref)
    gb_down[...] = jnp.zeros_like(gb_down)
    gb_out[...] = jnp.zeros_like(gb_out)
    gb_up[...] = jnp.zeros_like(gb_up)
    gb_qv[...] = jnp.zeros_like(gb_qv)

    def w_copies(p, m, slot):
        at, size = pieces[p]
        here = pl.ds(at, size)
        up_part, down_part = up_buf.at[slot, :, pl.ds(0, size)], down_buf.at[slot, pl.ds(0, size), :]
        return (
            Shard(own, w_all, 1, m, (slice(None), here), up_part, up_sem.at[slot]),
            Shard(own, w_all, 2, m, (here, slice(None)), down_part, down_sem.at[slot]),
        )

    for copy in w_copies(0, n - 1, 0):
        copy.start()

    def first(i, carry):
        at = rows_at(i, SLOT)
        col = item[at, :]
        middle = tokens[at, :].astype(f32) + pick(col, mod, 2) * branch_one[at, :]
        normed, _ = normal(middle)
        n_buf[at, :] = (normed * (1.0 + pick(col, mod, 4)) + pick(col, mod, 3)).astype(bf16)
        d = (pick(col, mod, 5) * upstream[at, :].astype(f32)).astype(bf16)
        d_buf[at, :] = d
        gb_down[...] += jnp.sum(d.astype(f32), axis=0, keepdims=True)
        acc_a[at, :] = jnp.broadcast_to(b_down[...], (SLOT, width))
        acc_b[at, :] = jnp.zeros((SLOT, width), f32)
        return carry

    lax.fori_loop(0, frames, first, 0)

    def flush(count, target, value):
        slot = count % 2
        size = value.shape[0]

        def copy(s):
            return pltpu.make_async_copy(
                stage_buf.at[s, pl.ds(0, size), :], target, stage_sem.at[s]
            )

        stage_buf[slot, pl.ds(0, size), :] = value.astype(bf16)
        dma = copy(slot)
        dma.start()
        dma.wait()

    for p, (p_at, p_size) in enumerate(pieces):

        def shard(i, carry, p=p, p_at=p_at, p_size=p_size):
            m = n - 1 - i
            slot = (p * n + i) % 2
            for copy in w_copies(p, m, slot):
                copy.wait()

            @pl.when(i + 1 < n)
            def _():
                for copy in w_copies(p, m - 1, 1 - slot):
                    copy.start()

            if p + 1 < len(pieces):

                @pl.when(i + 1 == n)
                def _():
                    for copy in w_copies(p + 1, n - 1, 1 - slot):
                        copy.start()

            bias = b_up[m, :, pl.ds(p_at, p_size)]
            up = up_buf.at[slot, :, pl.ds(0, p_size)]
            down = down_buf.at[slot, pl.ds(0, p_size), :]

            def part(j, c):
                at = rows_at(j, tile)
                pre = jnp.dot(n_buf[at, :], up[...], preferred_element_type=f32) + bias
                hidden, slope = gelu_both(pre)
                hidden = hidden.astype(bf16)
                dpre = nt(d_buf[at, :], down[...]) * slope
                dpre = dpre.astype(bf16)
                hid_buf[at, pl.ds(0, p_size)] = hidden
                dpre_buf[at, pl.ds(0, p_size)] = dpre
                gb_up[m, :, pl.ds(p_at, p_size)] += jnp.sum(
                    dpre.astype(f32), axis=0, keepdims=True
                )
                acc_a[at, :] += jnp.dot(hidden, down[...], preferred_element_type=f32)
                acc_b[at, :] += nt(dpre, up[...])
                return c

            lax.fori_loop(0, tiles, part, 0)
            flush(0, g_all.at[m, pl.ds(p_at, p_size), :], tn(hid_buf[:, pl.ds(0, p_size)], d_buf[...]))
            flush(1, g_all.at[m, pl.ds(ff + p_at, p_size), :], tn(dpre_buf[:, pl.ds(0, p_size)], n_buf[...]))
            return carry

        lax.fori_loop(0, n, shard, 0)

    def a_copies(m, slot):
        return (
            Shard(own, w_all, 0, m, slice(None), w_buf.at[slot], w_sem.at[slot]),
            pltpu.make_async_copy(qkv_hbm.at[m], qkv_buf.at[slot], qkv_sem.at[slot]),
            pltpu.make_async_copy(att_hbm.at[m], att_buf.at[slot], att_sem.at[slot]),
        )

    normed_copy = pltpu.make_async_copy(normed_hbm, n_buf, n_sem)
    normed_copy.start()
    for copy in a_copies(n - 1, 0):
        copy.start()

    def middle_part(i, carry):
        at = rows_at(i, SLOT)
        col = item[at, :]
        gate = pick(col, mod, 2)
        branch = branch_one[at, :]
        middle = tokens[at, :].astype(f32) + gate * branch
        dy = upstream[at, :].astype(f32)
        second = acc_a[at, :]
        output_ref[at, :] = (middle + pick(col, mod, 5) * second).astype(bf16)
        add_by_item(sums_ref, 5, col, dy * second)
        grad = acc_b[at, :]
        normed, rstd = normal(middle)
        add_by_item(sums_ref, 3, col, grad)
        add_by_item(sums_ref, 4, col, grad * normed)
        dmiddle = dy + normal_back(grad, pick(col, mod, 4), normed, rstd)
        acc_a[at, :] = dmiddle
        add_by_item(sums_ref, 2, col, dmiddle * branch)
        d = (gate * dmiddle).astype(bf16)
        d_buf[at, :] = d
        gb_out[...] += jnp.sum(d.astype(f32), axis=0, keepdims=True)
        acc_b[at, :] = jnp.zeros((SLOT, width), f32)
        return carry

    lax.fori_loop(0, frames, middle_part, 0)
    normed_copy.wait()

    def attn(i, carry):
        m = n - 1 - i
        slot = i % 2
        for copy in a_copies(m, slot):
            copy.wait()

        @pl.when(i + 1 < n)
        def _():
            for copy in a_copies(m - 1, 1 - slot):
                copy.start()

        def frame(f, c):
            at = rows_at(f, SLOT)
            datt = nt(w_buf[slot, pl.ds(3 * lw, lw), :], d_buf[at, :])
            pairs = pair_bias(ids[at, :], ids_row[pl.ds(f, 1), :])
            dqs, dks, dvs = [], [], []
            for h in range(heads):
                q = qkv_buf[slot, h, :, at]
                k = qkv_buf[slot, heads + h, :, at]
                v = qkv_buf[slot, 2 * heads + h, :, at]
                d = datt[h * HEAD : (h + 1) * HEAD].astype(bf16)
                scores = tn(k, q) * scale + pairs
                probs = jnp.exp(scores - lse[m, h : h + 1, at])
                dprobs = tn(v, d)
                inner = jnp.sum(dprobs * probs, axis=0, keepdims=True)
                dscores = (probs * (dprobs - inner)).astype(bf16)
                dvs.append(nt(d, probs.astype(bf16)))
                dqs.append(jnp.dot(k, dscores, preferred_element_type=f32) * scale)
                dks.append(nt(q, dscores) * scale)
            dproj = jnp.concatenate(dqs + dks + dvs, axis=0).astype(bf16)
            dproj_buf[:, at] = dproj
            gb_qv[m] += jnp.sum(dproj.astype(f32), axis=1, keepdims=True)
            acc_b[at, :] += tn(dproj, w_buf[slot, pl.ds(0, 3 * lw), :])
            return c

        lax.fori_loop(0, frames, frame, 0)
        flush(0, g_all.at[m, pl.ds(2 * ff + 3 * lw, lw), :], jnp.dot(att_buf[slot], d_buf[...], preferred_element_type=f32))
        for j in range(3):
            flush(1, g_all.at[m, pl.ds(2 * ff + j * lw, lw), :], jnp.dot(dproj_buf[pl.ds(j * lw, lw), :], n_buf[...], preferred_element_type=f32))
        return carry

    lax.fori_loop(0, n, attn, 0)

    def last(i, carry):
        at = rows_at(i, SLOT)
        col = item[at, :]
        normed, rstd = normal(tokens[at, :].astype(f32))
        grad = acc_b[at, :]
        add_by_item(sums_ref, 0, col, grad)
        add_by_item(sums_ref, 1, col, grad * normed)
        gtok_ref[at, :] = (
            acc_a[at, :] + normal_back(grad, pick(col, mod, 1), normed, rstd)
        ).astype(bf16)
        return carry

    lax.fori_loop(0, frames, last, 0)


def backward(tokens, upstream, branch_one, normed_one, item, ids, mod, b_up, b_down, lse, w_all, own, qkv, att):
    rows, width = tokens.shape
    n, ff = b_up.shape[0], b_up.shape[2]
    paired = bool(own)
    own = own or [w_all] * 3
    heads = qkv.shape[1] // 3
    lw = heads * HEAD
    pieces = pieces_of(ff)
    widest = max(size for _, size in pieces)
    tile = min(512, rows)
    vmem = pl.BlockSpec(memory_space=pltpu.VMEM)
    hbm = pl.BlockSpec(memory_space=pl.ANY)
    return pl.pallas_call(
        functools.partial(back_kernel, n, heads, pieces, tile, paired),
        out_shape=(
            jax.ShapeDtypeStruct((rows, width), bf16),
            jax.ShapeDtypeStruct((rows, width), bf16),
            jax.ShapeDtypeStruct(mod.shape, f32),
            jax.ShapeDtypeStruct((1, width), f32),
            jax.ShapeDtypeStruct((1, width), f32),
            jax.ShapeDtypeStruct((n, 1, ff), f32),
            jax.ShapeDtypeStruct((n, 3 * lw, 1), f32),
            jax.ShapeDtypeStruct((n, 2 * ff + 4 * lw, width), bf16),
        ),
        in_specs=[vmem] * 3 + [hbm] + [vmem] * 7 + [hbm] * 6,
        out_specs=(vmem,) * 7 + (hbm,),
        scratch_shapes=[
            pltpu.VMEM((rows, width), bf16),
            pltpu.VMEM((rows, width), bf16),
            pltpu.VMEM((rows, width), f32),
            pltpu.VMEM((rows, width), f32),
            pltpu.VMEM((2, width, widest), bf16),
            pltpu.VMEM((2, widest, width), bf16),
            pltpu.VMEM((2, 4 * lw, width), bf16),
            pltpu.VMEM((rows, widest), bf16),
            pltpu.VMEM((rows, widest), bf16),
            pltpu.VMEM((2, max(widest, lw), width), bf16),
            pltpu.VMEM((2, 3 * heads, HEAD, rows), bf16),
            pltpu.VMEM((2, lw, rows), bf16),
            pltpu.VMEM((3 * lw, rows), bf16),
            pltpu.SemaphoreType.DMA((2,)),
            pltpu.SemaphoreType.DMA((2,)),
            pltpu.SemaphoreType.DMA,
            pltpu.SemaphoreType.DMA((2,)),
            pltpu.SemaphoreType.DMA((2,)),
            pltpu.SemaphoreType.DMA((2,)),
            pltpu.SemaphoreType.DMA((2,)),
        ],
        compiler_params=pltpu.CompilerParams(vmem_limit_bytes=60 << 20),
    )(
        tokens, upstream, branch_one, normed_one, item[:, None], ids[:, None], ids.reshape(-1, SLOT),
        mod, b_up, b_down, lse, w_all, *own, qkv, att,
    )


def reduce_kernel(count, g_ref, tail_ref, out_ref, lp, rd, s0, sx, rx, tb, ry, ub, rz1, vb, rz2, ob, loads, sends, recvs, outs):
    dp, mp = lax.axis_index("dp"), lax.axis_index("mp")
    core, yb = mp % 2, dp % 2
    xb, z0, z1 = mp // 2, (dp // 2) % 2, dp // 4
    sib = (dp, mp + 1 - 2 * core)
    xn = (dp, mp + 2 - 4 * xb)
    yn = (dp + 1 - 2 * yb, mp)
    z1n = (dp + 2 - 4 * z0, mp)
    z2n = (dp + 4 - 8 * z1, mp)
    half, quarter, eighth = CHUNK // 2, CHUNK // 4, CHUNK // 8

    barrier = pltpu.get_barrier_semaphore()
    for peer in (sib, xn, yn, z1n, z2n):
        pl.semaphore_signal(barrier, inc=1, device_id=peer, device_id_type=MESH)
    pl.semaphore_wait(barrier, 5)

    def rows_of(c):
        return pl.ds(pl.multiple_of(c * CHUNK, CHUNK), CHUNK)

    def remote(stage, src, dst, peer, slot):
        return pltpu.make_async_remote_copy(
            src_ref=src,
            dst_ref=dst,
            send_sem=sends.at[stage, slot],
            recv_sem=recvs.at[stage, slot],
            device_id=peer,
            device_id_type=MESH,
        )

    main = g_ref.shape[1] // CHUNK

    def load(which, c, slot, ref):
        part = ref.at[2 * which, rows_of(c)]
        return pltpu.make_async_copy(part, lp.at[slot, which], loads.at[which, slot])

    def d_copy(which, c, slot, ref):
        return remote(which, ref.at[2 * which + 1, rows_of(c)], rd.at[slot, which], sib, slot)

    def x_copy(c, slot):
        return remote(2, sx.at[slot], rx.at[slot], xn, slot)

    def y_copy(c, slot):
        part = pl.ds(pl.multiple_of((1 - yb) * half, half), half)
        return remote(3, tb.at[slot, part], ry.at[slot], yn, slot)

    def z1_copy(c, slot):
        part = pl.ds(pl.multiple_of((1 - z0) * quarter, quarter), quarter)
        return remote(4, ub.at[slot, part], rz1.at[slot], z1n, slot)

    def z2_copy(c, slot):
        part = pl.ds(pl.multiple_of((1 - z1) * eighth, eighth), eighth)
        return remote(5, vb.at[slot, part], rz2.at[slot], z2n, slot)

    at_y = pl.multiple_of(yb * half, half)
    at_z1 = pl.multiple_of(yb * half + z0 * quarter, quarter)
    at_z2 = pl.multiple_of(yb * half + z0 * quarter + z1 * eighth, eighth)

    def back(stage, at, size, peer, c, slot):
        place = ob.at[c % OUT_SLOTS, pl.ds(at, size)]
        return remote(stage, place, place, peer, slot)

    def az2_copy(c, slot):
        return back(6, at_z2, eighth, z2n, c, slot)

    def az1_copy(c, slot):
        return back(7, at_z1, quarter, z1n, c, slot)

    def ay_copy(c, slot):
        return back(8, at_y, half, yn, c, slot)

    def out_copy(c, slot):
        return pltpu.make_async_copy(ob.at[c % OUT_SLOTS], out_ref.at[rows_of(c)], outs.at[slot])

    def step(i, carry):
        def stage(lag, work):
            c = i - lag

            @pl.when((c >= 0) & (c < count))
            def _():
                work(c, c % 2)

        def leave(c, slot):
            out_copy(c, slot).wait()

        def store(c, slot):
            ay_copy(c, slot).wait()
            out_copy(c, slot).start()

        def go_ay(c, slot):
            az1_copy(c, slot).wait()
            ay_copy(c, slot).start()

        def go_az1(c, slot):
            az2_copy(c, slot).wait()
            az1_copy(c, slot).start()

        def go_az2(c, slot):
            z2_copy(c, slot).wait()
            mine = vb[slot, pl.ds(pl.multiple_of(z1 * eighth, eighth), eighth)] + rz2[slot]
            ob[c % OUT_SLOTS, pl.ds(at_z2, eighth)] = mine
            az2_copy(c, slot).start()

        def go_z2(c, slot):
            z1_copy(c, slot).wait()
            vb[slot] = ub[slot, pl.ds(pl.multiple_of(z0 * quarter, quarter), quarter)] + rz1[slot]
            z2_copy(c, slot).start()

        def go_z1(c, slot):
            y_copy(c, slot).wait()
            ub[slot] = tb[slot, pl.ds(pl.multiple_of(yb * half, half), half)] + ry[slot]
            z1_copy(c, slot).start()

        def go_y(c, slot):
            x_copy(c, slot).wait()
            tb[slot] = s0[slot] + rx[slot]
            y_copy(c, slot).start()

        def go_x(c, slot):
            for which in range(2):
                load(which, 0, slot, g_ref).wait()
                d_copy(which, 0, slot, g_ref).wait()
            sx[slot] = lp[slot, 1] + rd[slot, 1]
            s0[slot] = lp[slot, 0] + rd[slot, 0]
            x_copy(c, slot).start()

        def go_d(c, slot):
            @pl.when(c < main)
            def _():
                for which in range(2):
                    load(which, c, slot, g_ref).start()
                    d_copy(which, c, slot, g_ref).start()

            @pl.when(c >= main)
            def _():
                for which in range(2):
                    load(which, c - main, slot, tail_ref).start()
                    d_copy(which, c - main, slot, tail_ref).start()

        stage(9, leave)
        stage(8, store)
        stage(7, go_ay)
        stage(6, go_az1)
        stage(5, go_az2)
        stage(4, go_z2)
        stage(3, go_z1)
        stage(2, go_y)
        stage(1, go_x)
        stage(0, go_d)
        return carry

    lax.fori_loop(0, count + 10, step, 0)


def reduce_grads(parts, tail):
    rows, width = parts.shape[1] + tail.shape[1], parts.shape[2]
    count = rows // CHUNK
    half, quarter, eighth = CHUNK // 2, CHUNK // 4, CHUNK // 8

    def buf(*lead):
        return pltpu.VMEM((*lead, width), bf16)

    return pl.pallas_call(
        functools.partial(reduce_kernel, count),
        out_shape=jax.ShapeDtypeStruct((rows, width), bf16),
        in_specs=[pl.BlockSpec(memory_space=pl.ANY)] * 2,
        out_specs=pl.BlockSpec(memory_space=pl.ANY),
        scratch_shapes=[
            buf(2, 2, CHUNK),
            buf(2, 2, CHUNK),
            buf(2, CHUNK),
            buf(2, CHUNK),
            buf(2, CHUNK),
            buf(2, CHUNK),
            buf(2, half),
            buf(2, half),
            buf(2, quarter),
            buf(2, quarter),
            buf(2, eighth),
            buf(OUT_SLOTS, CHUNK),
            pltpu.SemaphoreType.DMA((2, 2)),
            pltpu.SemaphoreType.DMA((9, 2)),
            pltpu.SemaphoreType.DMA((9, 2)),
            pltpu.SemaphoreType.DMA((2,)),
        ],
        compiler_params=pltpu.CompilerParams(
            collective_id=0, has_side_effects=True, vmem_limit_bytes=32 << 20
        ),
    )(parts, tail)


def swap(values, axis, bit):
    n = lax.axis_size(axis)
    return lax.ppermute(values, axis, [(i, i ^ bit) for i in range(n)])


def shards(
    paired,
    tokens,
    condition,
    grid_rows,
    grid_cols,
    frame_start,
    frame_item,
    group_frames,
    w_qkv,
    qv_bias,
    w_out,
    b_out,
    w_up,
    b_up,
    w_down,
    b_down,
    w_ada,
    b_ada,
    cotangent,
):
    own_rows, width = tokens.shape
    local_width = w_qkv.shape[2]
    local_ff = w_up.shape[1]
    items = condition.shape[0]
    n_mp, n_dp = lax.axis_size("mp"), lax.axis_size("dp")
    mp, dp = lax.axis_index("mp"), lax.axis_index("dp")
    n = width // (4 * HEAD)
    lw, ff = width // n, local_ff * n_mp // n
    frame_id, item_id = frame_tables(
        grid_rows, grid_cols, frame_start, frame_item, group_frames[0], mp * own_rows, own_rows
    )
    cond_value = condition.astype(f32)
    act_low = jax.nn.silu(cond_value).astype(bf16)
    ada_flat = w_ada.reshape(width, -1)
    ada_local = dot(act_low, ada_flat) + b_ada.reshape(-1).astype(f32)
    ada_local = ada_local.reshape(items, 6, local_width)
    qkv_local = w_qkv.transpose(1, 2, 0)
    if paired:
        qkv_bias = jnp.concatenate(
            [qv_bias[0].astype(f32), jnp.zeros((lw,), f32), qv_bias[1].astype(f32)]
        )
        small = jnp.concatenate([ada_local.reshape(-1), qkv_bias, b_up.astype(f32)])
        small = jnp.stack([small] + [swap(small, "mp", bit) for bit in range(1, n)])
        n_ada = ada_local.size
        modulation = small[mp ^ jnp.arange(n), :n_ada].reshape(n, items, 6, lw)
        qkv_bias = small[:, n_ada : n_ada + 3 * lw]
        up_bias = small[:, n_ada + 3 * lw :]
        weights = [
            jnp.concatenate([qkv_local.reshape(3 * lw, width), w_out], axis=0),
            w_up,
            w_down,
        ]
    else:
        modulation = lax.all_gather(ada_local, "mp", axis=0)
        qv = lax.all_gather(qv_bias.astype(f32), "mp", axis=1, tiled=True)
        qkv_bias = jnp.stack([qv[0], jnp.zeros((width,), f32), qv[1]])
        qkv_bias = qkv_bias.reshape(3, n, lw).transpose(1, 0, 2).reshape(n, 3 * lw)
        up_bias = lax.all_gather(b_up.astype(f32), "mp", axis=0, tiled=True).reshape(n, ff)
        qkv = lax.all_gather(qkv_local, "mp", axis=1, tiled=True)
        qkv = qkv.reshape(3, n, lw, width).transpose(1, 0, 2, 3).reshape(n, 3 * lw, width)
        out = lax.all_gather(w_out, "mp", axis=0, tiled=True).reshape(n, lw, width)
        up = lax.all_gather(w_up, "mp", axis=1, tiled=True)
        up = up.reshape(width, n, ff).transpose(1, 0, 2)
        down = lax.all_gather(w_down, "mp", axis=0, tiled=True).reshape(n, ff, width)
        weights = [jnp.stack([jnp.concatenate([qkv, out], axis=1), up, down])]
    modulation = modulation.transpose(1, 2, 0, 3).reshape(items, 6, width)
    b_out_row, b_down_row = (b.astype(f32)[None] for b in (b_out, b_down))
    normed_one, branch_one, qkv, lse, att, *gathered = attend(
        tokens, item_id, frame_id, modulation, qkv_bias[:, :, None], b_out_row, weights, paired
    )
    w_all = gathered[0] if paired else weights[0]
    output, grad_tokens, item_grad, gb_down, gb_out, gb_up, gb_qv, g_all = backward(
        tokens,
        cotangent,
        branch_one,
        normed_one,
        item_id,
        frame_id,
        modulation,
        up_bias[:, None],
        b_down_row,
        lse,
        w_all,
        weights if paired else [],
        qkv,
        att,
    )
    gb_qv = gb_qv.reshape(n, 3, lw)[:, ::2]

    if paired:
        item_grad = item_grad.reshape(items, 6, n, lw).transpose(2, 0, 1, 3)[mp ^ jnp.arange(n)]
        total_items = items * n_dp
        dmod_all = jnp.zeros((n, total_items, 6, lw), f32)
        dmod_all = lax.dynamic_update_slice(dmod_all, item_grad, (0, dp * items, 0, 0))
        act_all = jnp.zeros((total_items, width), f32)
        act_all = lax.dynamic_update_slice(act_all, act_low.astype(f32), (dp * items, 0))
        act_all = jnp.where(mp == 0, act_all, 0.0)
        fixed = jnp.concatenate([act_all, gb_out, gb_down])
        n_dmod = total_items * 6 * lw // width
        tail = jnp.concatenate(
            [
                dmod_all.reshape(n, n_dmod, width),
                jnp.broadcast_to(fixed[None], (n, *fixed.shape)),
                gb_up,
                jnp.pad(gb_qv.reshape(n, 1, 2 * lw), ((0, 0), (0, 0), (0, width - 2 * lw))),
            ],
            axis=1,
        )
        tail = jnp.pad(tail, ((0, 0), (0, -tail.shape[1] % CHUNK), (0, 0))).astype(bf16)
        total = reduce_grads(g_all, tail)
        tail = total[2 * ff + 4 * lw :].astype(f32)
        g_down, g_up = total[:ff].astype(f32), total[ff : 2 * ff].astype(f32).T
        g_qkv = total[2 * ff : 2 * ff + 3 * lw].astype(f32).T.reshape(width, 3, lw)
        g_out = total[2 * ff + 3 * lw : 2 * ff + 4 * lw].astype(f32)
        dmod = tail[:n_dmod].reshape(total_items, 6, lw)
        at = n_dmod
        act_all = tail[at : at + total_items]
        at = at + total_items
        gb_out, gb_down, gb_up = tail[at], tail[at + 1], tail[at + 2]
        gb_qv = tail[at + 3, : 2 * lw].reshape(2, lw)
        own_dmod = lax.dynamic_slice_in_dim(dmod, dp * items, items)
    else:

        def over_all(values, axis):
            part = lax.psum_scatter(values, "mp", scatter_dimension=axis, tiled=True)
            return lax.psum(part.astype(bf16), "dp").astype(f32)

        own_dmod = lax.psum_scatter(item_grad, "mp", scatter_dimension=2, tiled=True)
        dmod = lax.all_gather(own_dmod, "dp", axis=0, tiled=True)
        act_all = lax.all_gather(act_low, "dp", axis=0, tiled=True).astype(f32)
        g_down = over_all(g_all[:, :ff].reshape(n * ff, width), 0)
        g_up = over_all(g_all[:, ff : 2 * ff].reshape(n * ff, width).T, 1)
        g_qkv = g_all[:, 2 * ff : 2 * ff + 3 * lw].reshape(n, 3, lw, width)
        g_qkv = over_all(g_qkv.transpose(3, 1, 0, 2).reshape(width, 3, width), 2)
        g_out = over_all(g_all[:, 2 * ff + 3 * lw :].reshape(width, width), 0)
        gb_up = over_all(gb_up.reshape(-1), 0)
        gb_qv = over_all(gb_qv.transpose(1, 0, 2).reshape(2, width), 1)
        gb_out = lax.psum(gb_out[0], ("dp", "mp"))
        gb_down = lax.psum(gb_down[0], ("dp", "mp"))
    grad_w_ada = lax.dot_general(
        act_all,
        dmod.reshape(dmod.shape[0], -1),
        (((0,), (0,)), ((), ())),
        precision=lax.Precision.HIGHEST,
    ).reshape(width, 6, local_width)
    grad_b_ada = jnp.sum(dmod, axis=0)
    cond_term = lax.dot_general(
        own_dmod.reshape(items, -1),
        ada_flat.astype(f32),
        (((1,), (1,)), ((), ())),
        precision=lax.Precision.HIGHEST,
    )
    if paired:
        cond_term = cond_term + swap(cond_term, "mp", 1)
        cond_term = cond_term + swap(cond_term, "mp", 2)
    else:
        cond_term = lax.psum(cond_term, "mp")
    grad_condition = jax.vjp(jax.nn.silu, cond_value)[1](cond_term)[0]
    return (
        output,
        grad_tokens,
        grad_condition,
        g_qkv,
        gb_qv,
        g_out,
        gb_out,
        g_up,
        gb_up,
        g_down,
        gb_down,
        grad_w_ada,
        grad_b_ada,
    )


def solution(mesh):
    paired = dict(mesh.shape) == {"dp": 8, "mp": 4}
    return jax.shard_map(
        functools.partial(shards, paired),
        mesh=mesh,
        in_specs=(
            P(("dp", "mp"), None),
            P("dp", None),
            P("dp"),
            P("dp"),
            P("dp"),
            P("dp"),
            P("dp"),
            P(None, None, "mp"),
            P(None, "mp"),
            P("mp", None),
            P(),
            P(None, "mp"),
            P("mp"),
            P("mp", None),
            P(),
            P(None, None, "mp"),
            P(None, "mp"),
            P(("dp", "mp"), None),
        ),
        out_specs=(
            P(("dp", "mp"), None),
            P(("dp", "mp"), None),
            P("dp", None),
            P(None, None, "mp"),
            P(None, "mp"),
            P("mp", None),
            P(),
            P(None, "mp"),
            P("mp"),
            P("mp", None),
            P(),
            P(None, None, "mp"),
            P(None, "mp"),
        ),
        check_vma=False,
    )
```

time: 863 us -> 630 us (0.73); the launches traced: 854 us -> 630 us
  Pallas kernels: 236 us -> 569 us
  matrix products: 303 us -> 9.34 us
  other arithmetic: 130 us -> 16.7 us
  waiting for transfers between devices: 64.1 us -> 0.53 us
  local copies, waits for them, and re-layouts: 88.9 us -> 28.1 us
  between operations: 18.3 us -> 1.75 us
  starting transfers between devices: 13.5 us -> 3.95 us
    pallas_call x0 -> x2, Pallas kernels: none -> 331 us  [the longest x1 208 us: backward(): pl.pallas_call(functools.partial(back_kernel, n, heads, pieces, tile, pai...]
    dot_general x56 -> x0, matrix products: 201 us -> none  [the longest x16 88.5 us: col_inner(): lax.dot_general(left, right, (((1,), (1,)), ((), ())), preferred_element_...]
    dot_general x17 -> x1, matrix products: 95.9 us -> 3.29 us  [dot(): return jnp.dot(left, right, preferred_element_type=f32)]
    concatenate x10 -> x2, other arithmetic: 62.5 us -> 1.78 us  [the longest x1 1.71 us: shards(): jnp.concatenate([qkv_local.reshape(3 * lw, width), w_out], axis=0)]
    ppermute x18 -> x5, waiting for transfers between devices: 45.8 us -> 0.53 us  [swap(): return lax.ppermute(values, axis, [(i, i ^ bit) for i in range(n)])]
    reshape x23 -> x8, local copies, waits for them, and re-layouts: 33.1 us -> 1.85 us  [the longest x2 1.02 us: shards(): item_grad.reshape(items, 6, n, lw).transpose(2, 0, 1, 3)[mp ^ jnp.arange(n)]]
    convert_element_type x12 -> x3, other arithmetic: 28.9 us -> 6.23 us  [the longest x1 5.04 us: shards(): g_down, g_up = (total[:ff].astype(f32), total[ff:2 * ff].astype(f32).T)]
    unnamed x2 -> x0, waiting for transfers between devices: 18.3 us -> none
  transfers between devices with their start and end apart: 19 -> 5, of which waited for: 5 -> 1; matrix products, arithmetic and copies ran while one was open for 28% -> 2% of each run, Pallas kernels for 0% -> 0%
where the time goes in v2:
time: 630 us
  Pallas kernels  569 us (90%)
  local copies, waits for them, and re-layouts  28.1 us (4%)
  other arithmetic  16.7 us (3%)
  matrix products  9.34 us (1%)
    pallas_call x1, Pallas kernels, reduce_grads(): pl.pallas_call(functools.partial(reduce_kernel, count), out_shape=jax.Sha...  238 us
    pallas_call x1, Pallas kernels, backward(): pl.pallas_call(functools.partial(back_kernel, n, heads, pieces, tile, pai...  208 us
    pallas_call x1, Pallas kernels, attend(): pl.pallas_call(functools.partial(attend_kernel, n, heads, paired), out_sh...  123 us
  transfers between devices with their start and end apart: 5, of which 1 were waited for; matrix products, arithmetic and copies ran while one was open for 2% of the time, Pallas kernels for 0%

profile of v2, /device:TPU:0, one launch (start us, length us, event | category | flops | bytes accessed | tf_op | source)
XLA Modules:
  0.0 629.5 jit_solution(14129426069829134192)
XLA Ops:
  0.7 0.9 convert_reduce_fusion.1
  1.6 0.8 reshape.159
  2.4 3.3 convolution_add_fusion
  5.9 0.5 collective-permute-start
  6.3 2.6 collective-permute-start.1
  9.9 1.7 pad_maximum_fusion.refs_7_.own_attn
  11.7 0.6 sub.14.refs_3_.ids_row
  12.3 1.0 copy.52.refs_2_.ids
  13.3 1.0 copy.51.refs_1_.item
  14.3 0.6 reshape.162.refs_6_
  14.9 0.6 reshape.163.b_down
  15.8 8.9 %while.1 = (s32[]{:T(128)}, f32[4,5472]{1,0:T(4,128)S(1)}, s32[4,2]{0,1:T(2,128)S(1)}, f32[4,3456]{1,0:T(4,128)S(1)}, s32[]{:T(128)}, /*index=5*/s32[]{:T(128)}) while((s32[]{:T(128)}, f32[4,5472]{1,0:T(4,128)S(1)}, s32[4,2]{0,1:T(2,128)S(1)}, f32[4,3456]{1,0:T(4,128)S(1)}, s32[]{:T(128)}, /*index=5*/s32[]{:T(128)}) %tuple.34), condition=%wide.while_cond, body=%wide.while_body.sunk | while | flops 2 | bytes 55409 | solution.py:884
  15.9 0.5 fusion.20
  16.4 1.4 dynamic-slice.9
  17.8 0.2 dynamic-update-slice.4
  18.1 0.5 fusion.20
  18.6 1.4 dynamic-slice.9
  20.0 0.2 dynamic-update-slice.4
  20.3 0.5 fusion.20
  20.9 1.4 dynamic-slice.9
  22.2 0.2 dynamic-update-slice.4
  22.6 0.5 fusion.20
  23.1 1.4 dynamic-slice.9
  24.5 0.2 dynamic-update-slice.4
  24.9 0.7 reshape.179.refs_4_.mod
  25.6 1.8 copy.54.refs_5_
  27.4 0.6 broadcast_in_dim.73.b_up
  28.0 123.1 %shard_map.273 = (bf16[1024,1152]{1,0:T(8,128)(2,1)}, f32[1024,1152]{1,0:T(8,128)}, bf16[4,12,72,1024]{3,2,1,0:T(8,128)(2,1)}, f32[4,4,1024]{2,1,0:T(4,128)}, bf...) custom-call(bf16[1024,1152]{1,0:T(8,128)(2,1)} %tokens.1, s32[1024,1]{1,0:T(8,128)} %copy.51.refs_1_.item, ...), custom_call_target="tpu_custom_call" | custom-call | tf_op jit(solution)/shard_map/pallas_call | solution.py:344
  151.1 208.2 %shard_map.274 = (bf16[1024,1152]{1,0:T(8,128)(2,1)}, bf16[1024,1152]{1,0:T(8,128)(2,1)}, f32[2,6,1152]{2,1,0:T(8,128)}, f32[1,1152]{1,0:T(1,128)}, f32[1,1152]{...) custom-call(bf16[1024,1152]{1,0:T(8,128)(2,1)} %tokens.1, ...), custom_call_target="tpu_custom_call" | custom-call | tf_op jit(solution)/shard_map/pallas_call | solution.py:601
  359.3 1.0 reshape.177
  360.3 0.6 gather_fusion
  361.0 0.3 reshape.133
  361.3 2.0 convert_reduce_fusion
  363.6 0.7 convert.31
  364.3 0.7 maximum_convert_fusion
  365.2 237.8 %shard_map.275 = bf16[3584,1152]{1,0:T(8,128)(2,1)S(1)} custom-call(bf16[4,3456,1152]{2,1,0:T(8,128)(2,1)} %get-tuple-element.35.g_ref, bf16[4,128,1152]{2,1,0:T(8,128)(2,1)S(1)} %pad.12.tail_ref), custom_call_target="tpu_custom_call" | custom-call | tf_op jit(solution)/shard_map/pallas_call | solution.py:805
  603.0 5.0 slice_convert_fusion
  608.1 2.8 slice_convert_fusion.1
  610.9 1.1 slice_convert_fusion.2
  612.5 5.4 fusion.2
  617.9 0.6 convolution_bitcast_fusion
  618.6 0.6 slice_reduce_fusion
  619.3 0.5 collective-permute-done.3
  619.8 0.8 collective-permute-start.4
  620.6 6.9 %copy.64 = f32[1152,1152]{1,0:T(8,128)} copy(f32[1152,1152]{0,1:T(8,128)} %get-tuple-element.106) | data formatting | bytes 10616832
  627.6 0.6 reduce_sum.29
  628.2 0.7 reshape_squeeze.3
  628.9 0.6 fusion.11
  (80 shorter events, 2.3 us)
Async XLA Ops:
  0.6 5.1 copy-start.6
  0.7 9.0 %copy-start.10 = (s32[16]{0:T(128)S(1)}, s32[16]{0:T(128)}, u32[]{:S(2)}) copy-start(s32[16]{0:T(128)} %param.20) | copy-start | bytes 196
  0.7 9.0 %copy-start.11 = (s32[16]{0:T(128)S(1)}, s32[16]{0:T(128)}, u32[]{:S(2)}) copy-start(s32[16]{0:T(128)} %param.21) | copy-start | bytes 196
  0.7 9.0 %copy-start.9 = (s32[16]{0:T(128)S(1)}, s32[16]{0:T(128)}, u32[]{:S(2)}) copy-start(s32[16]{0:T(128)} %param.22) | copy-start | bytes 196
  0.7 9.0 %copy-start.12 = (s32[16]{0:T(128)S(1)}, s32[16]{0:T(128)}, u32[]{:S(2)}) copy-start(s32[16]{0:T(128)} %param.23) | copy-start | bytes 196
  0.7 9.2 %copy-start.2 = (bf16[1152,3,288]{0,2,1:T(8,128)(2,1)S(1)}, bf16[1152,3,288]{0,2,1:T(8,128)(2,1)}, u32[]{:S(2)}) copy-start(bf16[1152,3,288]{0,2,1:T(8,128)(2,1)} %param.25) | copy-start | bytes 5971972
  0.7 9.2 %copy-start.4 = (bf16[288,1152]{1,0:T(8,128)(2,1)S(1)}, bf16[288,1152]{1,0:T(8,128)(2,1)}, u32[]{:S(2)}) copy-start(bf16[288,1152]{1,0:T(8,128)(2,1)} %param.27) | copy-start | bytes 1990660
  2.4 9.2 %copy-start.5 = (bf16[2,1152]{1,0:T(2,128)(2,1)S(1)}, bf16[2,1152]{1,0:T(2,128)(2,1)}, u32[]{:S(2)}) copy-start(bf16[2,1152]{1,0:T(2,128)(2,1)} %param.19) | copy-start | bytes 13828
  5.7 8.7 %copy-start.7 = (bf16[1152]{0:T(1024)(128)(2,1)S(1)}, bf16[1152]{0:T(1024)(128)(2,1)}, u32[]{:S(2)}) copy-start(bf16[1152]{0:T(1024)(128)(2,1)} %param.28) | copy-start | bytes 6916
  5.7 9.3 %copy-start.8 = (bf16[1152]{0:T(1024)(128)(2,1)S(1)}, bf16[1152]{0:T(1024)(128)(2,1)}, u32[]{:S(2)}) copy-start(bf16[1152]{0:T(1024)(128)(2,1)} %param.32) | copy-start | bytes 6916
  5.9 9.7 %collective-permute-start = (f32[5472]{0:T(1024)S(1)}, f32[5472]{0:T(1024)S(1)}, u32[]{:S(2)}, u32[]{:S(2)}) collective-permute-start(f32[5472]{0:T(1024)S(1)} %concatenate.16), channel_id=1, source_target_pairs={{0,1},{1,0},{2,3},{3,2},{4,5},{5,4},{6,7},{7,6},{8,9},{9,8},{10,11... | collective-permute-start | bytes 65672 | tf_op jit(solution)/shard_map/ppermute | solution.py:836
  6.3 9.2 %collective-permute-start.1 = (f32[5472]{0:T(1024)S(1)}, f32[5472]{0:T(1024)S(1)}, u32[]{:S(2)}, u32[]{:S(2)}) collective-permute-start(f32[5472]{0:T(1024)S(1)} %concatenate.16), channel_id=1, source_target_pairs={{0,2},{1,3},{2,0},{3,1},{4,6},{5,7},{6,4},{7,5},{8,10},{9,11},{10,... | collective-permute-start | bytes 65672 | tf_op jit(solution)/shard_map/ppermute | solution.py:836
  8.9 6.7 %collective-permute-start.2 = (f32[5472]{0:T(1024)S(1)}, f32[5472]{0:T(1024)S(1)}, u32[]{:S(2)}, u32[]{:S(2)}) collective-permute-start(f32[5472]{0:T(1024)S(1)} %concatenate.16), channel_id=1, source_target_pairs={{0,3},{1,2},{2,1},{3,0},{4,7},{5,6},{6,5},{7,4},{8,11},{9,10},{10,... | collective-permute-start | bytes 65672 | tf_op jit(solution)/shard_map/ppermute | solution.py:836
  603.0 9.0 %copy-start = (bf16[3584,1152]{1,0:T(8,128)(2,1)}, bf16[3584,1152]{1,0:T(8,128)(2,1)S(1)}, u32[]{:S(2)}) copy-start(bf16[3584,1152]{1,0:T(8,128)(2,1)S(1)} %shard_map.275) | copy-start | bytes 24772612
  612.0 8.5 %copy-start.3 = (f32[128,1152]{1,0:T(8,128)}, f32[128,1152]{1,0:T(8,128)S(1)}, u32[]{:S(2)}) copy-start(f32[128,1152]{1,0:T(8,128)S(1)} %slice_convert_fusion.3) | copy-start | bytes 1769476
  612.5 5.4 copy-start.1
  618.5 1.2 collective-permute-start.3
  619.8 9.1 %collective-permute-start.4 = (f32[2,1152]{1,0:T(2,128)S(1)}, f32[2,1152]{1,0:T(2,128)S(1)}, u32[]{:S(2)}, u32[]{:S(2)}) collective-permute-start(f32[2,1152]{1,0:T(2,128)S(1)} %add.84), channel_id=1, source_target_pairs={{0,2},{1,3},{2,0},{3,1},{4,6},{5,7},{6,4},{7,5},{8,10},{9,11},{10,... | collective-permute-start | bytes 27656 | tf_op jit(solution)/shard_map/ppermute | solution.py:836
  620.6 6.9 %slice-start = ((f32[128,1152]{1,0:T(8,128)}), f32[24,1152]{1,0:T(8,128)S(1)}, s32[]{:S(2)}) async-start(f32[128,1152]{1,0:T(8,128)} %copy-done.3), calls=%async_computation | async-start | bytes 221184 | tf_op jit(solution)/shard_map/slice | solution.py:954

commit v3 on v2

--- a/solution.py
+++ b/solution.py
@@ -45,12 +45,6 @@
 
 def dot(left, right):
     return jnp.dot(left, right, preferred_element_type=f32)
-
-
-def pieces_of(ff):
-    if ff % 128 or ff <= 640:
-        return [(0, ff)]
-    return [(0, 640), (640, ff - 640)]
 
 
 def rows_at(i, size):
@@ -381,14 +375,229 @@
     return v * half, slope
 
 
-def back_kernel(
-    n, heads, pieces, tile, paired,
-    tokens, upstream, branch_one, normed_hbm, item, ids, ids_row, mod, b_up, b_down, lse,
-    w_all, own_attn, own_up, own_down, qkv_hbm, att_hbm,
-    output_ref, gtok_ref, sums_ref, gb_down, gb_out, gb_up, gb_qv, g_all,
-    n_buf, d_buf, acc_a, acc_b, up_buf, down_buf, w_buf, hid_buf, dpre_buf, stage_buf, qkv_buf, att_buf, dproj_buf,
-    up_sem, down_sem, n_sem, stage_sem, w_sem, qkv_sem, att_sem,
-):
+def pieces_of(ff):
+    if ff != 1152:
+        return [(0, ff)]
+    return [(0, 256), (256, 384), (640, 512)]
+
+
+def stream_of(ff, lw):
+    at, downs, ups = 0, [], []
+    for _, size in pieces_of(ff):
+        downs.append(at)
+        ups.append(at + size)
+        at += 2 * size
+    return downs, ups, at, at + lw
+
+
+def split_stream(rows, ff, lw):
+    downs, ups, out_row, qkv_row = stream_of(ff, lw)
+    sizes = [size for _, size in pieces_of(ff)]
+    down, up = (
+        jnp.concatenate([rows[at : at + size] for at, size in zip(starts, sizes)])
+        for starts in (downs, ups)
+    )
+    return down, up, rows[out_row:qkv_row], rows[qkv_row : qkv_row + 3 * lw]
+
+
+X_RUNS = ((2, 0, 4), (6, 4, 6), (12, 10, 8), (20, 18, 2), (23, 20, 7))
+L_RUNS = ((4, 0, 4), (8, 4, 6), (16, 10, 8), (24, 18, 2), (27, 20, 7))
+LAST_TICK = 34 + 8
+
+
+def in_runs(tick, runs):
+    chunk, inside = 0, False
+    for start, first, size in runs:
+        here = (tick >= start) & (tick < start + size)
+        chunk = jnp.where(here, first + tick - start, chunk)
+        inside = here | inside
+    return chunk, inside
+
+
+class Reduction:
+    def __init__(self, d_in, s_own, s_far, x_in, out_ref, lp, tb, ry, ub, rz1, vb, rz2, ob, dsend, drecv, xsend, xrecv, loads, sends, recvs, outs):
+        self.d_in, self.s_own, self.s_far, self.x_in, self.out_ref = d_in, s_own, s_far, x_in, out_ref
+        self.lp, self.tb, self.ry, self.ub, self.rz1, self.vb, self.rz2, self.ob = lp, tb, ry, ub, rz1, vb, rz2, ob
+        self.dsend, self.drecv, self.xsend, self.xrecv = dsend, drecv, xsend, xrecv
+        self.loads, self.sends, self.recvs, self.outs = loads, sends, recvs, outs
+        dp, mp = lax.axis_index("dp"), lax.axis_index("mp")
+        core, self.yb = mp % 2, dp % 2
+        xb, self.z0, self.z1 = mp // 2, (dp // 2) % 2, dp // 4
+        self.sib = (dp, mp + 1 - 2 * core)
+        self.xn = (dp, mp + 2 - 4 * xb)
+        self.yn = (dp + 1 - 2 * self.yb, mp)
+        self.z1n = (dp + 2 - 4 * self.z0, mp)
+        self.z2n = (dp + 4 - 8 * self.z1, mp)
+
+    def greet(self):
+        barrier = pltpu.get_barrier_semaphore()
+        for peer in (self.sib, self.xn, self.yn, self.z1n, self.z2n):
+            pl.semaphore_signal(barrier, inc=1, device_id=peer, device_id_type=MESH)
+        pl.semaphore_wait(barrier, 5)
+
+    def to_sibling(self, which, flush, source, row, size):
+        return pltpu.make_async_remote_copy(
+            src_ref=source,
+            dst_ref=self.d_in.at[which, pl.ds(row, size)],
+            send_sem=self.dsend.at[which, flush],
+            recv_sem=self.drecv.at[which, flush],
+            device_id=self.sib,
+            device_id_type=MESH,
+        )
+
+    def x_copy(self, c):
+        return pltpu.make_async_remote_copy(
+            src_ref=self.s_far.at[rows_at(c, CHUNK)],
+            dst_ref=self.x_in.at[rows_at(c, CHUNK)],
+            send_sem=self.xsend.at[c],
+            recv_sem=self.xrecv.at[c],
+            device_id=self.xn,
+            device_id_type=MESH,
+        )
+
+    def tick(self, tick):
+        yb, z0, z1 = self.yb, self.z0, self.z1
+        half, quarter, eighth = CHUNK // 2, CHUNK // 4, CHUNK // 8
+        at_y = pl.multiple_of(yb * half, half)
+        at_z1 = pl.multiple_of(yb * half + z0 * quarter, quarter)
+        at_z2 = pl.multiple_of(yb * half + z0 * quarter + z1 * eighth, eighth)
+        lp, tb, ub, vb, ob = self.lp, self.tb, self.ub, self.vb, self.ob
+
+        def remote(stage, slot, src, dst, peer):
+            return pltpu.make_async_remote_copy(
+                src_ref=src,
+                dst_ref=dst,
+                send_sem=self.sends.at[stage, slot],
+                recv_sem=self.recvs.at[stage, slot],
+                device_id=peer,
+                device_id_type=MESH,
+            )
+
+        def load(which, c):
+            source = (self.s_own, self.x_in)[which].at[rows_at(c, CHUNK)]
+            return pltpu.make_async_copy(source, lp.at[c % 2, which], self.loads.at[which, c % 2])
+
+        def y_copy(c):
+            part = rows_at(1 - yb, half)
+            return remote(0, c % 2, tb.at[c % 2, part], self.ry.at[c % 2], self.yn)
+
+        def z1_copy(c):
+            part = rows_at(1 - z0, quarter)
+            return remote(1, c % 2, ub.at[c % 2, part], self.rz1.at[c % 2], self.z1n)
+
+        def z2_copy(c):
+            part = rows_at(1 - z1, eighth)
+            return remote(2, c % 2, vb.at[c % 2, part], self.rz2.at[c % 2], self.z2n)
+
+        def back(stage, c, at, size, peer):
+            place = ob.at[c % OUT_SLOTS, pl.ds(at, size)]
+            return remote(stage, c % 2, place, place, peer)
+
+        def az2_copy(c):
+            return back(3, c, at_z2, eighth, self.z2n)
+
+        def az1_copy(c):
+            return back(4, c, at_z1, quarter, self.z1n)
+
+        def ay_copy(c):
+            return back(5, c, at_y, half, self.yn)
+
+        def out_copy(c):
+            return pltpu.make_async_copy(
+                ob.at[c % OUT_SLOTS], self.out_ref.at[rows_at(c, CHUNK)], self.outs.at[c % 2]
+            )
+
+        def stage(lag, work):
+            c, inside = in_runs(tick - lag, L_RUNS)
+
+            @pl.when(inside)
+            def _():
+                work(c)
+
+        def leave(c):
+            out_copy(c).wait()
+
+        def store(c):
+            ay_copy(c).wait()
+            out_copy(c).start()
+
+        def go_ay(c):
+            az1_copy(c).wait()
+            ay_copy(c).start()
+
+        def go_az1(c):
+            az2_copy(c).wait()
+            az1_copy(c).start()
+
+        def go_az2(c):
+            z2_copy(c).wait()
+            ob[c % OUT_SLOTS, pl.ds(at_z2, eighth)] = vb[c % 2, rows_at(z1, eighth)] + self.rz2[c % 2]
+            az2_copy(c).start()
+
+        def go_z2(c):
+            z1_copy(c).wait()
+            vb[c % 2] = ub[c % 2, rows_at(z0, quarter)] + self.rz1[c % 2]
+            z2_copy(c).start()
+
+        def go_z1(c):
+            y_copy(c).wait()
+            ub[c % 2] = tb[c % 2, rows_at(yb, half)] + self.ry[c % 2]
+            z1_copy(c).start()
+
+        def go_y(c):
+            for which in range(2):
+                load(which, c).wait()
+            tb[c % 2] = lp[c % 2, 0] + lp[c % 2, 1]
+            y_copy(c).start()
+
+        def go_load(c):
+            self.x_copy(c).wait()
+            for which in range(2):
+                load(which, c).start()
+
+        stage(8, leave)
+        stage(7, store)
+        stage(6, go_ay)
+        stage(5, go_az1)
+        stage(4, go_az2)
+        stage(3, go_z2)
+        stage(2, go_z1)
+        stage(1, go_y)
+        stage(0, go_load)
+        c, inside = in_runs(tick, X_RUNS)
+
+        @pl.when(inside)
+        def _():
+            self.x_copy(c).start()
+
+
+N_RED = 21
+
+
+def back_kernel(n, heads, tile, paired, *refs):
+    (
+        tokens, upstream, branch_one, normed_hbm, item, ids, ids_row, mod, b_up, b_down, lse,
+        w_all, own_attn, own_up, own_down, qkv_hbm, att_hbm,
+        output_hbm, gtok_hbm, sums_ref, gb_down, gb_out, gb_up, gb_qv, *refs,
+    ) = refs
+    if paired:
+        *shared, (
+            n_buf, d_buf, acc_a, acc_b, up_buf, down_buf, w_buf, hid_buf, dpre_buf, stage_buf, qkv_buf, att_buf, datt_buf, dproj_buf,
+            up_sem, down_sem, n_sem, stage_sem, w_sem, qkv_sem, att_sem,
+        ) = (*refs[:5], refs[5:26])
+        r_buf, r_sem, *more = refs[26:]
+        red = Reduction(*shared, *more)
+        red.greet()
+        tick = red.tick
+    else:
+        (
+            g_all, n_buf, d_buf, acc_a, acc_b, up_buf, down_buf, w_buf, hid_buf, dpre_buf, stage_buf, qkv_buf, att_buf, datt_buf, dproj_buf,
+            up_sem, down_sem, n_sem, stage_sem, w_sem, qkv_sem, att_sem,
+        ) = refs
+
+        def tick(t):
+            pass
+
     rows, width = tokens.shape
     lw = heads * HEAD
     frames = rows // SLOT
@@ -396,11 +605,68 @@
     tiles = rows // tile
     own = (own_attn, own_up, own_down) if paired else None
     ff = w_all.shape[2]
+    pieces = pieces_of(ff)
+    downs, ups, out_row, qkv_row = stream_of(ff, lw)
     sums_ref[...] = jnp.zeros_like(sums_ref)
     gb_down[...] = jnp.zeros_like(gb_down)
     gb_out[...] = jnp.zeros_like(gb_out)
     gb_up[...] = jnp.zeros_like(gb_up)
-    gb_qv[...] = jnp.zeros_like(gb_qv)
+
+    def landed(m, blocks):
+        if not paired:
+            return
+
+        @pl.when(m % 2 == 0)
+        def _():
+            for slot, (flush, row, size) in enumerate(blocks):
+                stage = stage_buf.at[slot, pl.ds(0, size)]
+                sent = red.to_sibling(m // 2, flush, stage, row, size)
+                sent.wait()
+                fetch(m // 2, slot, row, size).start()
+
+    def fetch(which, slot, row, size):
+        return pltpu.make_async_copy(
+            red.d_in.at[which, pl.ds(row, size)], r_buf.at[slot, pl.ds(0, size)], r_sem.at[slot]
+        )
+
+    def put(target, slot, row, size):
+        return pltpu.make_async_copy(
+            stage_buf.at[slot, pl.ds(0, size)], target.at[pl.ds(row, size)], stage_sem.at[slot]
+        )
+
+    def settle(blocks):
+        if paired:
+            for slot, (flush, row, size) in enumerate(blocks):
+                put(red.s_own, slot, row, size).wait()
+
+    def leave(m, slot, block, value):
+        flush, row, size = block
+        if not paired:
+            stage_buf[slot, pl.ds(0, size), :] = value.astype(bf16)
+            copy = put(g_all.at[m], slot, row, size)
+            copy.start()
+            copy.wait()
+            return
+
+        @pl.when(m % 2 == 1)
+        def _():
+            stage_buf[slot, pl.ds(0, size), :] = value.astype(bf16)
+            stage = stage_buf.at[slot, pl.ds(0, size)]
+            red.to_sibling(m // 2, flush, stage, row, size).start()
+
+        @pl.when(m % 2 == 0)
+        def _():
+            fetch(m // 2, slot, row, size).wait()
+            total = value + r_buf[slot, pl.ds(0, size), :].astype(f32)
+            stage_buf[slot, pl.ds(0, size), :] = total.astype(bf16)
+
+            @pl.when(m == 0)
+            def _():
+                put(red.s_own, slot, row, size).start()
+
+            @pl.when(m > 0)
+            def _():
+                put(red.s_far, slot, row, size).start()
 
     def w_copies(p, m, slot):
         at, size = pieces[p]
@@ -429,23 +695,15 @@
 
     lax.fori_loop(0, frames, first, 0)
 
-    def flush(count, target, value):
-        slot = count % 2
-        size = value.shape[0]
-
-        def copy(s):
-            return pltpu.make_async_copy(
-                stage_buf.at[s, pl.ds(0, size), :], target, stage_sem.at[s]
-            )
-
-        stage_buf[slot, pl.ds(0, size), :] = value.astype(bf16)
-        dma = copy(slot)
-        dma.start()
-        dma.wait()
-
+    def blocks_of(p):
+        size = pieces[p][1]
+        return ((2 * p, downs[p], size), (2 * p + 1, ups[p], size))
+
+    now = 0
     for p, (p_at, p_size) in enumerate(pieces):
-
-        def shard(i, carry, p=p, p_at=p_at, p_size=p_size):
+        beats = 2 if p_size > 384 else 1
+
+        def shard(i, carry, p=p, p_at=p_at, p_size=p_size, beats=beats, now=now):
             m = n - 1 - i
             slot = (p * n + i) % 2
             for copy in w_copies(p, m, slot):
@@ -463,6 +721,7 @@
                     for copy in w_copies(p + 1, n - 1, 1 - slot):
                         copy.start()
 
+            blocks = blocks_of(p)
             bias = b_up[m, :, pl.ds(p_at, p_size)]
             up = up_buf.at[slot, :, pl.ds(0, p_size)]
             down = down_buf.at[slot, pl.ds(0, p_size), :]
@@ -484,23 +743,60 @@
                 return c
 
             lax.fori_loop(0, tiles, part, 0)
-            flush(0, g_all.at[m, pl.ds(p_at, p_size), :], tn(hid_buf[:, pl.ds(0, p_size)], d_buf[...]))
-            flush(1, g_all.at[m, pl.ds(ff + p_at, p_size), :], tn(dpre_buf[:, pl.ds(0, p_size)], n_buf[...]))
+
+            @pl.when(i == 2)
+            def _():
+                settle(blocks)
+
+            if p:
+
+                @pl.when(i == 0)
+                def _():
+                    settle(blocks_of(p - 1))
+
+            tick(now + beats * i)
+            landed(m, blocks)
+            leave(m, 0, blocks[0], tn(hid_buf[:, pl.ds(0, p_size)], d_buf[...]))
+            leave(m, 1, blocks[1], tn(dpre_buf[:, pl.ds(0, p_size)], n_buf[...]))
+            if beats > 1:
+                tick(now + beats * i + 1)
             return carry
 
         lax.fori_loop(0, n, shard, 0)
+        now += n * beats
+    settle(blocks_of(len(pieces) - 1))
 
     def a_copies(m, slot):
         return (
             Shard(own, w_all, 0, m, slice(None), w_buf.at[slot], w_sem.at[slot]),
             pltpu.make_async_copy(qkv_hbm.at[m], qkv_buf.at[slot], qkv_sem.at[slot]),
-            pltpu.make_async_copy(att_hbm.at[m], att_buf.at[slot], att_sem.at[slot]),
         )
+
+    def att_copy(m, slot):
+        return pltpu.make_async_copy(att_hbm.at[m], att_buf.at[slot], att_sem.at[slot])
 
     normed_copy = pltpu.make_async_copy(normed_hbm, n_buf, n_sem)
     normed_copy.start()
     for copy in a_copies(n - 1, 0):
         copy.start()
+    att_copy(n - 1, 0).start()
+
+    def row_copy(target, i):
+        return pltpu.make_async_copy(
+            stage_buf.at[i % 2, pl.ds(0, SLOT)], target.at[rows_at(i, SLOT)], stage_sem.at[i % 2]
+        )
+
+    def row_out(target, i, value):
+        @pl.when(i >= 2)
+        def _():
+            row_copy(target, i - 2).wait()
+
+        stage_buf[i % 2, pl.ds(0, SLOT), :] = value.astype(bf16)
+        row_copy(target, i).start()
+
+    def rows_done(target):
+        for i in range(max(frames - 2, 0), frames):
+            row_copy(target, i).wait()
 
     def middle_part(i, carry):
         at = rows_at(i, SLOT)
@@ -510,7 +806,7 @@
         middle = tokens[at, :].astype(f32) + gate * branch
         dy = upstream[at, :].astype(f32)
         second = acc_a[at, :]
-        output_ref[at, :] = (middle + pick(col, mod, 5) * second).astype(bf16)
+        row_out(output_hbm, i, middle + pick(col, mod, 5) * second)
         add_by_item(sums_ref, 5, col, dy * second)
         grad = acc_b[at, :]
         normed, rstd = normal(middle)
@@ -523,10 +819,42 @@
         d_buf[at, :] = d
         gb_out[...] += jnp.sum(d.astype(f32), axis=0, keepdims=True)
         acc_b[at, :] = jnp.zeros((SLOT, width), f32)
+
+        @pl.when(i % 2 == 1)
+        def _():
+            tick(now + i // 2)
+
         return carry
 
     lax.fori_loop(0, frames, middle_part, 0)
+    rows_done(output_hbm)
+    now += 2
     normed_copy.wait()
+    out_block = (2 * len(pieces), out_row, lw)
+
+    def out_part(i, carry):
+        m = n - 1 - i
+        slot = i % 2
+        att_copy(m, slot).wait()
+
+        @pl.when(i + 1 < n)
+        def _():
+            att_copy(m - 1, 1 - slot).start()
+
+        @pl.when(i == 2)
+        def _():
+            settle((out_block,))
+
+        landed(m, (out_block,))
+        leave(m, 0, out_block, jnp.dot(att_buf[slot], d_buf[...], preferred_element_type=f32))
+        return carry
+
+    lax.fori_loop(0, n, out_part, 0)
+    settle((out_block,))
+    tick(now)
+    now += 1
+    some = 3 * lw // 2
+    qkv_blocks = tuple((2 * len(pieces) + 1 + j, qkv_row + j * some, some) for j in range(2))
 
     def attn(i, carry):
         m = n - 1 - i
@@ -539,16 +867,19 @@
             for copy in a_copies(m - 1, 1 - slot):
                 copy.start()
 
+        datt = nt(w_buf[slot, pl.ds(3 * lw, lw), :], d_buf[...])
+        for h in range(heads):
+            datt_buf[h] = datt[h * HEAD : (h + 1) * HEAD].astype(bf16)
+
         def frame(f, c):
             at = rows_at(f, SLOT)
-            datt = nt(w_buf[slot, pl.ds(3 * lw, lw), :], d_buf[at, :])
             pairs = pair_bias(ids[at, :], ids_row[pl.ds(f, 1), :])
             dqs, dks, dvs = [], [], []
             for h in range(heads):
                 q = qkv_buf[slot, h, :, at]
                 k = qkv_buf[slot, heads + h, :, at]
                 v = qkv_buf[slot, 2 * heads + h, :, at]
-                d = datt[h * HEAD : (h + 1) * HEAD].astype(bf16)
+                d = datt_buf[h, :, at]
                 scores = tn(k, q) * scale + pairs
                 probs = jnp.exp(scores - lse[m, h : h + 1, at])
                 dprobs = tn(v, d)
@@ -557,19 +888,34 @@
                 dvs.append(nt(d, probs.astype(bf16)))
                 dqs.append(jnp.dot(k, dscores, preferred_element_type=f32) * scale)
                 dks.append(nt(q, dscores) * scale)
-            dproj = jnp.concatenate(dqs + dks + dvs, axis=0).astype(bf16)
-            dproj_buf[:, at] = dproj
-            gb_qv[m] += jnp.sum(dproj.astype(f32), axis=1, keepdims=True)
-            acc_b[at, :] += tn(dproj, w_buf[slot, pl.ds(0, 3 * lw), :])
+            dproj_buf[:, at] = jnp.concatenate(dqs + dks + dvs, axis=0).astype(bf16)
             return c
 
         lax.fori_loop(0, frames, frame, 0)
-        flush(0, g_all.at[m, pl.ds(2 * ff + 3 * lw, lw), :], jnp.dot(att_buf[slot], d_buf[...], preferred_element_type=f32))
-        for j in range(3):
-            flush(1, g_all.at[m, pl.ds(2 * ff + j * lw, lw), :], jnp.dot(dproj_buf[pl.ds(j * lw, lw), :], n_buf[...], preferred_element_type=f32))
+
+        @pl.when(i == 2)
+        def _():
+            settle(qkv_blocks)
+
+        tick(now + 2 * i)
+        landed(m, qkv_blocks)
+        gb_qv[m] = jnp.sum(dproj_buf[...].astype(f32), axis=1, keepdims=True)
+        for j, block in enumerate(qkv_blocks):
+            part = dproj_buf[pl.ds(j * some, some), :]
+            leave(m, j, block, jnp.dot(part, n_buf[...], preferred_element_type=f32))
+
+        def part(j, c):
+            at = rows_at(j, tile)
+            acc_b[at, :] += tn(dproj_buf[:, at], w_buf[slot, pl.ds(0, 3 * lw), :])
+            return c
+
+        lax.fori_loop(0, tiles, part, 0)
+        tick(now + 2 * i + 1)
         return carry
 
     lax.fori_loop(0, n, attn, 0)
+    settle(qkv_blocks)
+    now += 2 * n
 
     def last(i, carry):
         at = rows_at(i, SLOT)
@@ -578,28 +924,74 @@
         grad = acc_b[at, :]
         add_by_item(sums_ref, 0, col, grad)
         add_by_item(sums_ref, 1, col, grad * normed)
-        gtok_ref[at, :] = (
-            acc_a[at, :] + normal_back(grad, pick(col, mod, 1), normed, rstd)
-        ).astype(bf16)
+        row_out(gtok_hbm, i, acc_a[at, :] + normal_back(grad, pick(col, mod, 1), normed, rstd))
+
+        @pl.when(i == 1)
+        def _():
+            tick(now)
+
         return carry
 
     lax.fori_loop(0, frames, last, 0)
+    rows_done(gtok_hbm)
+    if paired:
+
+        def drain(t, carry):
+            tick(t)
+            return carry
+
+        lax.fori_loop(now + 1, LAST_TICK + 1, drain, 0)
 
 
 def backward(tokens, upstream, branch_one, normed_one, item, ids, mod, b_up, b_down, lse, w_all, own, qkv, att):
     rows, width = tokens.shape
     n, ff = b_up.shape[0], b_up.shape[2]
+    heads = qkv.shape[1] // 3
+    lw = heads * HEAD
     paired = bool(own)
     own = own or [w_all] * 3
-    heads = qkv.shape[1] // 3
-    lw = heads * HEAD
     pieces = pieces_of(ff)
     widest = max(size for _, size in pieces)
     tile = min(512, rows)
+    total = 2 * ff + 4 * lw
+    deep = max(widest, 3 * lw // 2, SLOT)
+    slots = 2
+    flushes = 2 * len(pieces) + 3
+    half, quarter, eighth = CHUNK // 2, CHUNK // 4, CHUNK // 8
     vmem = pl.BlockSpec(memory_space=pltpu.VMEM)
     hbm = pl.BlockSpec(memory_space=pl.ANY)
+    dma = pltpu.SemaphoreType.DMA
+
+    def buf(*shape):
+        return pltpu.VMEM(shape, bf16)
+
+    grads = [jax.ShapeDtypeStruct((n, total, width), bf16)]
+    extra = []
+    if paired:
+        grads = [jax.ShapeDtypeStruct((2, total, width), bf16)]
+        grads += [jax.ShapeDtypeStruct((total, width), bf16)] * 4
+        extra = [
+            buf(slots, deep, width),
+            dma((slots,)),
+            buf(2, 2, CHUNK, width),
+            buf(2, CHUNK, width),
+            buf(2, half, width),
+            buf(2, half, width),
+            buf(2, quarter, width),
+            buf(2, quarter, width),
+            buf(2, eighth, width),
+            buf(OUT_SLOTS, CHUNK, width),
+            dma((2, flushes)),
+            dma((2, flushes)),
+            dma((total // CHUNK,)),
+            dma((total // CHUNK,)),
+            dma((2, 2)),
+            dma((6, 2)),
+            dma((6, 2)),
+            dma((2,)),
+        ]
     return pl.pallas_call(
-        functools.partial(back_kernel, n, heads, pieces, tile, paired),
+        functools.partial(back_kernel, n, heads, tile, paired),
         out_shape=(
             jax.ShapeDtypeStruct((rows, width), bf16),
             jax.ShapeDtypeStruct((rows, width), bf16),
@@ -608,33 +1000,37 @@
             jax.ShapeDtypeStruct((1, width), f32),
             jax.ShapeDtypeStruct((n, 1, ff), f32),
             jax.ShapeDtypeStruct((n, 3 * lw, 1), f32),
-            jax.ShapeDtypeStruct((n, 2 * ff + 4 * lw, width), bf16),
+            *grads,
         ),
         in_specs=[vmem] * 3 + [hbm] + [vmem] * 7 + [hbm] * 6,
-        out_specs=(vmem,) * 7 + (hbm,),
+        out_specs=(hbm,) * 2 + (vmem,) * 5 + (hbm,) * len(grads),
         scratch_shapes=[
-            pltpu.VMEM((rows, width), bf16),
-            pltpu.VMEM((rows, width), bf16),
+            buf(rows, width),
+            buf(rows, width),
             pltpu.VMEM((rows, width), f32),
             pltpu.VMEM((rows, width), f32),
-            pltpu.VMEM((2, width, widest), bf16),
-            pltpu.VMEM((2, widest, width), bf16),
-            pltpu.VMEM((2, 4 * lw, width), bf16),
-            pltpu.VMEM((rows, widest), bf16),
-            pltpu.VMEM((rows, widest), bf16),
-            pltpu.VMEM((2, max(widest, lw), width), bf16),
-            pltpu.VMEM((2, 3 * heads, HEAD, rows), bf16),
-            pltpu.VMEM((2, lw, rows), bf16),
-            pltpu.VMEM((3 * lw, rows), bf16),
-            pltpu.SemaphoreType.DMA((2,)),
-            pltpu.SemaphoreType.DMA((2,)),
-            pltpu.SemaphoreType.DMA,
-            pltpu.SemaphoreType.DMA((2,)),
-            pltpu.SemaphoreType.DMA((2,)),
-            pltpu.SemaphoreType.DMA((2,)),
-            pltpu.SemaphoreType.DMA((2,)),
+            buf(2, width, widest),
+            buf(2, widest, width),
+            buf(2, 4 * lw, width),
+            buf(rows, widest),
+            buf(rows, widest),
+            buf(slots, deep, width),
+            buf(2, 3 * heads, HEAD, rows),
+            buf(2, lw, rows),
+            buf(heads, HEAD, rows),
+            buf(3 * lw, rows),
+            dma((2,)),
+            dma((2,)),
+            dma,
+            dma((slots,)),
+            dma((2,)),
+            dma((2,)),
+            dma((2,)),
+            *extra,
         ],
-        compiler_params=pltpu.CompilerParams(vmem_limit_bytes=60 << 20),
+        compiler_params=pltpu.CompilerParams(
+            collective_id=2 if paired else None, has_side_effects=paired, vmem_limit_bytes=63 << 20
+        ),
     )(
         tokens, upstream, branch_one, normed_one, item[:, None], ids[:, None], ids.reshape(-1, SLOT),
         mod, b_up, b_down, lse, w_all, *own, qkv, att,
@@ -795,7 +1191,7 @@
 
 
 def reduce_grads(parts, tail):
-    rows, width = parts.shape[1] + tail.shape[1], parts.shape[2]
+    rows, width = parts.shape[1], parts.shape[2]
     count = rows // CHUNK
     half, quarter, eighth = CHUNK // 2, CHUNK // 4, CHUNK // 8
 
@@ -908,7 +1304,7 @@
         tokens, item_id, frame_id, modulation, qkv_bias[:, :, None], b_out_row, weights, paired
     )
     w_all = gathered[0] if paired else weights[0]
-    output, grad_tokens, item_grad, gb_down, gb_out, gb_up, gb_qv, g_all = backward(
+    output, grad_tokens, item_grad, gb_down, gb_out, gb_up, gb_qv, *grads = backward(
         tokens,
         cotangent,
         branch_one,
@@ -946,11 +1342,10 @@
             axis=1,
         )
         tail = jnp.pad(tail, ((0, 0), (0, -tail.shape[1] % CHUNK), (0, 0))).astype(bf16)
-        total = reduce_grads(g_all, tail)
-        tail = total[2 * ff + 4 * lw :].astype(f32)
-        g_down, g_up = total[:ff].astype(f32), total[ff : 2 * ff].astype(f32).T
-        g_qkv = total[2 * ff : 2 * ff + 3 * lw].astype(f32).T.reshape(width, 3, lw)
-        g_out = total[2 * ff + 3 * lw : 2 * ff + 4 * lw].astype(f32)
+        tail = reduce_grads(tail, tail).astype(f32)
+        g_down, g_up, g_out, g_qkv = split_stream(grads[4], ff, lw)
+        g_down, g_out = g_down.astype(f32), g_out.astype(f32)
+        g_up, g_qkv = g_up.astype(f32).T, g_qkv.astype(f32).T.reshape(width, 3, lw)
         dmod = tail[:n_dmod].reshape(total_items, 6, lw)
         at = n_dmod
         act_all = tail[at : at + total_items]
@@ -967,11 +1362,12 @@
         own_dmod = lax.psum_scatter(item_grad, "mp", scatter_dimension=2, tiled=True)
         dmod = lax.all_gather(own_dmod, "dp", axis=0, tiled=True)
         act_all = lax.all_gather(act_low, "dp", axis=0, tiled=True).astype(f32)
-        g_down = over_all(g_all[:, :ff].reshape(n * ff, width), 0)
-        g_up = over_all(g_all[:, ff : 2 * ff].reshape(n * ff, width).T, 1)
-        g_qkv = g_all[:, 2 * ff : 2 * ff + 3 * lw].reshape(n, 3, lw, width)
-        g_qkv = over_all(g_qkv.transpose(3, 1, 0, 2).reshape(width, 3, width), 2)
-        g_out = over_all(g_all[:, 2 * ff + 3 * lw :].reshape(width, width), 0)
+        g_down, g_up, g_out, g_qkv = jax.vmap(lambda g: split_stream(g, ff, lw))(grads[0])
+        g_down = over_all(g_down.reshape(n * ff, width), 0)
+        g_up = over_all(g_up.reshape(n * ff, width).T, 1)
+        g_qkv = g_qkv.reshape(n, 3, lw, width).transpose(3, 1, 0, 2).reshape(width, 3, width)
+        g_qkv = over_all(g_qkv, 2)
+        g_out = over_all(g_out.reshape(width, width), 0)
         gb_up = over_all(gb_up.reshape(-1), 0)
         gb_qv = over_all(gb_qv.transpose(1, 0, 2).reshape(2, width), 1)
         gb_out = lax.psum(gb_out[0], ("dp", "mp"))

time: 630 us -> 536 us (0.85); the launches traced: 630 us -> 527 us
  Pallas kernels: 569 us -> 444 us
  local copies, waits for them, and re-layouts: 28.1 us -> 48.3 us
    pallas_call x1, Pallas kernels: 238 us -> 35.4 us  [reduce_grads(): pl.pallas_call(functools.partial(reduce_kernel, count), out_shape=jax.Sha...]
    pallas_call x1, Pallas kernels: 208 us -> 285 us  [backward(): pl.pallas_call(functools.partial(back_kernel, n, heads, tile, paired), ou...]
    slice x0 -> x3, local copies, waits for them, and re-layouts: none -> 6.66 us  [split_stream(): rows[at:at + size]]
  transfers between devices with their start and end apart: 5 -> 5, of which waited for: 1 -> 0; matrix products, arithmetic and copies ran while one was open for 2% -> 4% of each run, Pallas kernels for 0% -> 0%
where the time goes in v3:
time: 536 us; the launch traced here: 527 us
  Pallas kernels  444 us (83%)
  local copies, waits for them, and re-layouts  48.3 us (9%)
  other arithmetic  19.9 us (4%)
  matrix products  9.46 us (2%)
    pallas_call x1, Pallas kernels, backward(): pl.pallas_call(functools.partial(back_kernel, n, heads, tile, paired), ou...  285 us
    pallas_call x1, Pallas kernels, attend(): pl.pallas_call(functools.partial(attend_kernel, n, heads, paired), out_sh...  123 us
    pallas_call x1, Pallas kernels, reduce_grads(): pl.pallas_call(functools.partial(reduce_kernel, count), out_shape=jax.Sha...  35.4 us
    unnamed x37, local copies, waits for them, and re-layouts  11.6 us
  transfers between devices with their start and end apart: 5, of which 0 were waited for; matrix products, arithmetic and copies ran while one was open for 4% of the time, Pallas kernels for 0%

profile of v3, /device:TPU:0, one launch (start us, length us, event | category | flops | bytes accessed | tf_op | source)
XLA Modules:
  0.0 527.0 jit_solution(661352841788927072)
XLA Ops:
  0.7 0.9 convert_reduce_fusion.1
  1.6 0.8 reshape.159
  2.4 3.3 convolution_add_fusion
  6.3 2.6 collective-permute-start.1
  9.9 1.7 pad_maximum_fusion.refs_7_.refs_12_
  12.3 1.0 copy.52.refs_2_.refs_5_
  13.3 1.0 copy.51.refs_1_.refs_4_
  15.8 8.9 %while.1 = (s32[]{:T(128)}, f32[4,5472]{1,0:T(4,128)S(1)}, s32[4,2]{0,1:T(2,128)S(1)}, f32[4,3456]{1,0:T(4,128)S(1)}, s32[]{:T(128)}, /*index=5*/s32[]{:T(128)}) while((s32[]{:T(128)}, f32[4,5472]{1,0:T(4,128)S(1)}, s32[4,2]{0,1:T(2,128)S(1)}, f32[4,3456]{1,0:T(4,128)S(1)}, s32[]{:T(128)}, /*index=5*/s32[]{:T(128)}) %tuple.36), condition=%wide.while_cond, body=%wide.while_body.sunk | while | flops 2 | bytes 55409 | solution.py:1280
  16.4 1.4 dynamic-slice.9
  18.6 1.4 dynamic-slice.9
  20.9 1.4 dynamic-slice.9
  23.1 1.4 dynamic-slice.9
  24.9 0.7 reshape.179.refs_4_.refs_7_
  25.6 1.8 copy.54.refs_5_
  27.4 0.6 broadcast_in_dim.73.refs_8_
  28.0 123.1 %shard_map.273 = (bf16[1024,1152]{1,0:T(8,128)(2,1)}, f32[1024,1152]{1,0:T(8,128)}, bf16[4,12,72,1024]{3,2,1,0:T(8,128)(2,1)}, f32[4,4,1024]{2,1,0:T(4,128)}, bf...) custom-call(bf16[1024,1152]{1,0:T(8,128)(2,1)} %refs_0_.3, s32[1024,1]{1,0:T(8,128)} %copy.51.refs_1_.refs_4_, ...), custom_call_target="tpu_custom_call" | custom-call | tf_op jit(solution)/shard_map/pallas_call | solution.py:338
  151.1 285.3 %shard_map.274 = (bf16[1024,1152]{1,0:T(8,128)(2,1)}, bf16[1024,1152]{1,0:T(8,128)(2,1)}, f32[2,6,1152]{2,1,0:T(8,128)}, f32[1,1152]{1,0:T(1,128)}, f32[1,1152]{...) custom-call(bf16[1024,1152]{1,0:T(8,128)(2,1)} %refs_0_.3, ...), custom_call_target="tpu_custom_call" | custom-call | tf_op jit(solution)/shard_map/pallas_call | solution.py:993
  436.4 1.8 fusion.19
  438.3 2.5 fusion.18
  440.8 2.3 fusion.17
  443.3 0.6 gather_fusion
  443.9 0.8 broadcast_in_dim.76
  444.7 0.6 copy_dynamic-update-slice_fusion
  445.3 1.3 reshape.133
  446.6 2.0 convert_reduce_fusion
  448.9 0.7 convert.31
  449.6 0.7 maximum_convert_fusion.1
  450.5 35.4 %shard_map.275 = bf16[128,1152]{1,0:T(8,128)(2,1)S(1)} custom-call(bf16[4,128,1152]{2,1,0:T(8,128)(2,1)S(1)} %pad.12.g_ref.tail_ref, bf16[4,128,1152]{2,1,0:T(8,128)(2,1)S(1)} %pad.12.g_ref.tail_ref), custom_call_target="tpu_custom_call" | custom-call | tf_op jit(solution)/shard_map/pallas_call | solution.py:1201
  485.9 0.6 slice.65
  486.6 0.9 convert_element_type.63
  487.4 1.6 reshape_reshape.7
  489.0 1.6 reshape.136
  490.6 3.7 slice_convert_fusion
  494.3 2.2 slice_convert_fusion.1
  496.6 1.6 dot_general.16
  498.2 5.5 %fusion.2 = f32[1152,6,288]{0,2,1:T(8,128)} fusion(bf16[6,288,16]{1,0,2:T(8,128)(2,1)} %dot_general.16, bf16[128,1152]{1,0:T(8,128)(2,1)S(1)} %shard_map.275), kind=kOutput, calls=%fused_computation.17 | convolution fusion | flops 63700992 | bytes 8054784 | tf_op jit(solution)/shard_map/dot_general | solution.py:1375
  503.7 0.8 constant_dynamic-slice_fusion.1
  504.5 0.6 convolution_bitcast_fusion
  505.3 2.7 maximum_convert_fusion
  508.0 2.7 convert_bitcast_fusion
  510.7 1.5 slice_reduce_fusion
  512.3 0.7 slice_reduce_fusion.3
  513.0 6.9 %copy.64 = f32[1152,1152]{1,0:T(8,128)} copy(f32[1152,1152]{0,1:T(8,128)} %convert_bitcast_fusion) | data formatting | bytes 10616832
  519.9 0.7 reshape_squeeze.3
  520.7 0.6 reduce_sum.29
  521.3 0.6 fusion.11
  521.9 3.2 copy.89
  525.2 1.4 copy.90
  (93 shorter events, 7.2 us)
Async XLA Ops:
  0.6 5.1 copy-start.10
  0.7 9.0 %copy-start.14 = (s32[16]{0:T(128)S(1)}, s32[16]{0:T(128)}, u32[]{:S(2)}) copy-start(s32[16]{0:T(128)} %param.20) | copy-start | bytes 196
  0.7 9.0 %copy-start.15 = (s32[16]{0:T(128)S(1)}, s32[16]{0:T(128)}, u32[]{:S(2)}) copy-start(s32[16]{0:T(128)} %param.21) | copy-start | bytes 196
  0.7 9.0 %copy-start.13 = (s32[16]{0:T(128)S(1)}, s32[16]{0:T(128)}, u32[]{:S(2)}) copy-start(s32[16]{0:T(128)} %param.22) | copy-start | bytes 196
  0.7 9.0 %copy-start.16 = (s32[16]{0:T(128)S(1)}, s32[16]{0:T(128)}, u32[]{:S(2)}) copy-start(s32[16]{0:T(128)} %param.23) | copy-start | bytes 196
  0.7 9.2 %copy-start.5 = (bf16[1152,3,288]{0,2,1:T(8,128)(2,1)S(1)}, bf16[1152,3,288]{0,2,1:T(8,128)(2,1)}, u32[]{:S(2)}) copy-start(bf16[1152,3,288]{0,2,1:T(8,128)(2,1)} %param.25) | copy-start | bytes 5971972
  0.7 9.2 %copy-start.6 = (bf16[288,1152]{1,0:T(8,128)(2,1)S(1)}, bf16[288,1152]{1,0:T(8,128)(2,1)}, u32[]{:S(2)}) copy-start(bf16[288,1152]{1,0:T(8,128)(2,1)} %param.27) | copy-start | bytes 1990660
  2.4 9.2 %copy-start.8 = (bf16[2,1152]{1,0:T(2,128)(2,1)S(1)}, bf16[2,1152]{1,0:T(2,128)(2,1)}, u32[]{:S(2)}) copy-start(bf16[2,1152]{1,0:T(2,128)(2,1)} %param.19) | copy-start | bytes 13828
  5.7 8.7 %copy-start.11 = (bf16[1152]{0:T(1024)(128)(2,1)S(1)}, bf16[1152]{0:T(1024)(128)(2,1)}, u32[]{:S(2)}) copy-start(bf16[1152]{0:T(1024)(128)(2,1)} %param.28) | copy-start | bytes 6916
  5.7 9.3 %copy-start.12 = (bf16[1152]{0:T(1024)(128)(2,1)S(1)}, bf16[1152]{0:T(1024)(128)(2,1)}, u32[]{:S(2)}) copy-start(bf16[1152]{0:T(1024)(128)(2,1)} %param.32) | copy-start | bytes 6916
  5.9 9.7 %collective-permute-start = (f32[5472]{0:T(1024)S(1)}, f32[5472]{0:T(1024)S(1)}, u32[]{:S(2)}, u32[]{:S(2)}) collective-permute-start(f32[5472]{0:T(1024)S(1)} %concatenate.22), channel_id=1, source_target_pairs={{0,1},{1,0},{2,3},{3,2},{4,5},{5,4},{6,7},{7,6},{8,9},{9,8},{10,11... | collective-permute-start | bytes 65672 | tf_op jit(solution)/shard_map/ppermute | solution.py:1232
  6.3 9.2 %collective-permute-start.1 = (f32[5472]{0:T(1024)S(1)}, f32[5472]{0:T(1024)S(1)}, u32[]{:S(2)}, u32[]{:S(2)}) collective-permute-start(f32[5472]{0:T(1024)S(1)} %concatenate.22), channel_id=1, source_target_pairs={{0,2},{1,3},{2,0},{3,1},{4,6},{5,7},{6,4},{7,5},{8,10},{9,11},{10,... | collective-permute-start | bytes 65672 | tf_op jit(solution)/shard_map/ppermute | solution.py:1232
  8.9 6.7 %collective-permute-start.2 = (f32[5472]{0:T(1024)S(1)}, f32[5472]{0:T(1024)S(1)}, u32[]{:S(2)}, u32[]{:S(2)}) collective-permute-start(f32[5472]{0:T(1024)S(1)} %concatenate.22), channel_id=1, source_target_pairs={{0,3},{1,2},{2,1},{3,0},{4,7},{5,6},{6,5},{7,4},{8,11},{9,10},{10,... | collective-permute-start | bytes 65672 | tf_op jit(solution)/shard_map/ppermute | solution.py:1232
  438.3 4.9 copy-start.7
  438.3 11.4 %copy-start.9 = (f32[1,1152]{1,0:T(1,128)S(1)}, f32[1,1152]{1,0:T(1,128)}, u32[]{:S(2)}) copy-start(f32[1,1152]{1,0:T(1,128)} %get-tuple-element.37) | copy-start | bytes 13828
  498.2 6.4 %copy-start = (bf16[1152,6,288]{0,2,1:T(8,128)(2,1)S(1)}, bf16[1152,6,288]{0,2,1:T(8,128)(2,1)}, u32[]{:S(2)}) copy-start(bf16[1152,6,288]{0,2,1:T(8,128)(2,1)} %param.33) | copy-start | bytes 11943940
  503.7 1.5 copy-start.1
  503.7 1.6 copy-start.4
  505.2 7.0 %collective-permute-start.3 = (f32[2,1152]{1,0:T(2,128)S(1)}, f32[2,1152]{1,0:T(2,128)S(1)}, u32[]{:S(2)}, u32[]{:S(2)}) collective-permute-start(f32[2,1152]{1,0:T(2,128)S(1)} %convolution_bitcast_fusion), channel_id=1, source_target_pairs={{0,1},{1,0},{2,3},{3,2},{4,5},{5,4},{6,7},{7,6},{8,9},{9,8},{10,11... | collective-permute-start | bytes 27656 | tf_op jit(solution)/shard_map/ppermute | solution.py:1232
  505.3 2.7 copy-start.3
  512.2 9.1 %collective-permute-start.4 = (f32[2,1152]{1,0:T(2,128)S(1)}, f32[2,1152]{1,0:T(2,128)S(1)}, u32[]{:S(2)}, u32[]{:S(2)}) collective-permute-start(f32[2,1152]{1,0:T(2,128)S(1)} %add.84), channel_id=1, source_target_pairs={{0,2},{1,3},{2,0},{3,1},{4,6},{5,7},{6,4},{7,5},{8,10},{9,11},{10,... | collective-permute-start | bytes 27656 | tf_op jit(solution)/shard_map/ppermute | solution.py:1232
  519.9 5.3 %copy-start.2 = (bf16[1024,1152]{1,0:T(8,128)(2,1)S(1)}, bf16[1024,1152]{1,0:T(8,128)(2,1)}, u32[]{:S(2)}) copy-start(bf16[1024,1152]{1,0:T(8,128)(2,1)} %get-tuple-element.174) | copy-start | bytes 7077892
